TPU v7x, 256 devices: a whole 4x4x8 slice. The times are simulated.
256 devices in a mesh: gx: 16 (over z_lo, x), gy: 16 (over y, z_hi, core).
Axes of the slice: x: 4, y: 4, z: 8 (z_hi: 2, z_lo: 4; z = z_hi * 4 + z_lo), core: 2. Of those that a mesh axis runs over, the one named last changes fastest.
Arguments:
- field: bfloat16 [64, 128, 1024], P('gx', 'gy'), may hold values from -6 to 6
- cotangent: bfloat16 [64, 128, 1024], P('gx', 'gy'), may hold values from -6 to 6
- kernel_one: bfloat16 [27, 32, 32], replicated, may hold values from -0.21875 to 0.21875
- kernel_two: bfloat16 [27, 32, 32], replicated, may hold values from -0.21875 to 0.21875
- spectral_weight: float32 [2, 4608, 32, 32], P(None, ('gx', 'gy')), may hold values from -9 to 9
Outputs:
- field_grad: bfloat16 [64, 128, 1024], P('gx', 'gy')
- kernel_one_grad: float32 [27, 32, 32], replicated
- kernel_two_grad: float32 [27, 32, 32], replicated
- spectral_grad: float32 [2, 4608, 32, 32], P(None, ('gx', 'gy'))
All inputs are finite; a program needn't handle non-finite values.
Results may differ from a plain program's by a relative error of at most 0.0055.
Values may be sent and summed in bfloat16 or wider, within the bound.
A program may use at most 128 MiB of HBM per device.

v0:
```python
import math

import jax
import jax.numpy as jnp
from jax import lax
from jax.sharding import PartitionSpec as P

C = 32
MX = 24
MY = 24
MZ = 8
NZ = 32


HIGH = lax.Precision.HIGHEST


def with_halo(cells, sides, width):
    for axis, dim in sides:
        count = lax.axis_size(axis)
        ends = count - 1
        head = lax.slice_in_dim(cells, 0, width, axis=dim)
        tail = lax.slice_in_dim(cells, cells.shape[dim] - width, cells.shape[dim], axis=dim)
        cells = jnp.concatenate(
            [
                lax.ppermute(tail, axis, [(i, (i + 1) % count) for i in range(ends)]),
                cells,
                lax.ppermute(head, axis, [((i + 1) % count, i) for i in range(ends)]),
            ],
            axis=dim,
        )
    return cells


def phase(coords, freqs, length):
    turns = coords[:, None] * freqs[None, :] % length
    angle = turns.astype(jnp.float32) * (2.0 * math.pi / length)
    return (jnp.cos(angle), jnp.sin(angle))


def kept(length, count):
    half = count // 2
    return jnp.concatenate(
        [jnp.arange(half, dtype=jnp.int32), length - half + jnp.arange(half, dtype=jnp.int32)]
    )


def tables(xs, ys, nx, ny):
    cos_x, sin_x = phase(xs, kept(nx, MX), nx)
    cos_y, sin_y = phase(ys, kept(ny, MY), ny)
    cos_z, sin_z = phase(jnp.arange(NZ, dtype=jnp.int32), jnp.arange(MZ, dtype=jnp.int32), NZ)
    return (cos_x, sin_x, cos_y, sin_y, cos_z, sin_z)


def analyse(field32, tabs):
    cos_x, sin_x, cos_y, sin_y, cos_z, sin_z = tabs
    zre = jnp.einsum("xyzc,zk->xykc", field32, cos_z, precision=HIGH)
    zim = -jnp.einsum("xyzc,zk->xykc", field32, sin_z, precision=HIGH)
    yre = jnp.einsum("xykc,yj->xjkc", zre, cos_y, precision=HIGH) + jnp.einsum(
        "xykc,yj->xjkc", zim, sin_y, precision=HIGH
    )
    yim = jnp.einsum("xykc,yj->xjkc", zim, cos_y, precision=HIGH) - jnp.einsum(
        "xykc,yj->xjkc", zre, sin_y, precision=HIGH
    )
    are = jnp.einsum("xjkc,xi->ikjc", yre, cos_x, precision=HIGH) + jnp.einsum(
        "xjkc,xi->ikjc", yim, sin_x, precision=HIGH
    )
    aim = jnp.einsum("xjkc,xi->ikjc", yim, cos_x, precision=HIGH) - jnp.einsum(
        "xjkc,xi->ikjc", yre, sin_x, precision=HIGH
    )
    return (are.reshape(-1, field32.shape[3]), aim.reshape(-1, field32.shape[3]))


def synthesise(real_part, imag_part, tabs):
    cos_x, sin_x, cos_y, sin_y, cos_z, sin_z = tabs
    are = real_part.reshape(MX, MZ, MY, -1)
    aim = imag_part.reshape(MX, MZ, MY, -1)
    bre = jnp.einsum("ikjc,xi->xjkc", are, cos_x, precision=HIGH) - jnp.einsum(
        "ikjc,xi->xjkc", aim, sin_x, precision=HIGH
    )
    bim = jnp.einsum("ikjc,xi->xjkc", aim, cos_x, precision=HIGH) + jnp.einsum(
        "ikjc,xi->xjkc", are, sin_x, precision=HIGH
    )
    cre = jnp.einsum("xjkc,yj->xykc", bre, cos_y, precision=HIGH) - jnp.einsum(
        "xjkc,yj->xykc", bim, sin_y, precision=HIGH
    )
    cim = jnp.einsum("xjkc,yj->xykc", bim, cos_y, precision=HIGH) + jnp.einsum(
        "xjkc,yj->xykc", bre, sin_y, precision=HIGH
    )
    return jnp.einsum("xykc,zk->xyzc", cre, cos_z, precision=HIGH) - jnp.einsum(
        "xykc,zk->xyzc", cim, sin_z, precision=HIGH
    )


def mode_scale(modes, ncells):
    kz = modes // MY % MZ
    return (jnp.where(kz == 0, 1.0, 2.0) / ncells).astype(jnp.float32)[:, None]


def pad_depth(values):
    return jnp.pad(values, ((0, 0), (0, 0), (1, 1), (0, 0)))


def conv_sum(padded, kernel, len_x, len_y):
    total = jnp.zeros((len_x * len_y * NZ, kernel.shape[2]), jnp.float32)
    for offset in range(27):
        a, b, e = (offset // 9, offset // 3 % 3, offset % 3)
        piece = padded[a : a + len_x, b : b + len_y, e : e + NZ].reshape(-1, kernel.shape[1])
        total = total + jnp.dot(piece, kernel[offset], preferred_element_type=jnp.float32)
    return total.reshape(len_x, len_y, NZ, kernel.shape[2])


def conv_back(padded, kernel, len_x, len_y):
    total = jnp.zeros((len_x * len_y * NZ, kernel.shape[1]), jnp.float32)
    for offset in range(27):
        a, b, e = (offset // 9, offset // 3 % 3, offset % 3)
        piece = padded[2 - a : 2 - a + len_x, 2 - b : 2 - b + len_y, 2 - e : 2 - e + NZ].reshape(
            -1, kernel.shape[2]
        )
        total = total + jnp.dot(piece, kernel[offset].T, preferred_element_type=jnp.float32)
    return total.reshape(len_x, len_y, NZ, kernel.shape[1])


def correlate(padded, grad, len_x, len_y):
    flat_grad = grad.reshape(-1, grad.shape[3])
    terms = []
    for offset in range(27):
        a, b, e = (offset // 9, offset // 3 % 3, offset % 3)
        piece = padded[a : a + len_x, b : b + len_y, e : e + NZ].reshape(-1, padded.shape[3])
        terms.append(jnp.dot(piece.T, flat_grad, preferred_element_type=jnp.float32))
    return jnp.stack(terms)


def mix_modes(xre, xim, wre, wim):
    yre = jnp.einsum("mi,mio->mo", xre, wre, precision=HIGH) - jnp.einsum(
        "mi,mio->mo", xim, wim, precision=HIGH
    )
    yim = jnp.einsum("mi,mio->mo", xre, wim, precision=HIGH) + jnp.einsum(
        "mi,mio->mo", xim, wre, precision=HIGH
    )
    return (yre, yim)


def weight_grads(xre, xim, dyre, dyim, wre, wim):
    gre = jnp.einsum("mi,mo->mio", xre, dyre, precision=HIGH) + jnp.einsum(
        "mi,mo->mio", xim, dyim, precision=HIGH
    )
    gim = jnp.einsum("mi,mo->mio", xre, dyim, precision=HIGH) - jnp.einsum(
        "mi,mo->mio", xim, dyre, precision=HIGH
    )
    dxre = jnp.einsum("mio,mo->mi", wre, dyre, precision=HIGH) + jnp.einsum(
        "mio,mo->mi", wim, dyim, precision=HIGH
    )
    dxim = jnp.einsum("mio,mo->mi", wre, dyim, precision=HIGH) - jnp.einsum(
        "mio,mo->mi", wim, dyre, precision=HIGH
    )
    return (jnp.stack([gre, gim]), dxre, dxim)


def spectrum_of(values, tabs):
    are, aim = analyse(values, tabs)
    owned_rows = lax.psum_scatter(
        jnp.concatenate([are, aim], axis=1), ("gx", "gy"), scatter_dimension=0, tiled=True
    )
    return (owned_rows[:, :C], owned_rows[:, C:])


def field_of(real_part, imag_part, tabs):
    packed = jnp.concatenate([real_part, imag_part], axis=1)
    whole_rows = lax.all_gather(packed, ("gx", "gy"), axis=0, tiled=True)
    return synthesise(whole_rows[:, :C], whole_rows[:, C:], tabs)


def shards(field, cotangent, kernel_one, kernel_two, spectral_weight):
    len_x = field.shape[0]
    len_y = field.shape[1]
    nx = len_x * lax.axis_size("gx")
    ny = len_y * lax.axis_size("gy")
    xs = lax.axis_index("gx") * len_x + jnp.arange(len_x, dtype=jnp.int32)
    ys = lax.axis_index("gy") * len_y + jnp.arange(len_y, dtype=jnp.int32)
    tabs = tables(xs, ys, nx, ny)
    owned_count = spectral_weight.shape[1]
    first_mode = (lax.axis_index("gx") * lax.axis_size("gy") + lax.axis_index("gy")) * owned_count
    scale = mode_scale(first_mode + jnp.arange(owned_count, dtype=jnp.int32), nx * ny * NZ)
    width = 1
    rimmed = with_halo(field, (("gx", 0), ("gy", 1)), width)
    inputs = field.reshape(len_x, len_y, NZ, C)
    padded_x = pad_depth(rimmed.reshape(len_x + 2, len_y + 2, NZ, C))
    pre = conv_sum(padded_x, kernel_one, len_x, len_y)
    hidden = jax.nn.gelu(pre).astype(jnp.bfloat16)
    hidden_rim = with_halo(hidden.reshape(len_x, len_y, NZ * C), (("gx", 0), ("gy", 1)), 1)
    padded_h = pad_depth(hidden_rim.reshape(len_x + 2, len_y + 2, NZ, C))
    branch = conv_sum(padded_h, kernel_two, len_x, len_y)
    xre, xim = spectrum_of(inputs.astype(jnp.float32), tabs)
    yre, yim = mix_modes(xre, xim, spectral_weight[0], spectral_weight[1])
    total = field_of(yre * scale, yim * scale, tabs) + branch
    _, pull = jax.vjp(jax.nn.gelu, total)
    dtotal = pull(cotangent.reshape(len_x, len_y, NZ, C).astype(jnp.float32))[0].astype(
        jnp.bfloat16
    )
    dtotal_rim = with_halo(dtotal.reshape(len_x, len_y, NZ * C), (("gx", 0), ("gy", 1)), width)
    padded_dz = pad_depth(dtotal_rim.reshape(len_x + 2, len_y + 2, NZ, C))
    dhidden = conv_back(padded_dz, kernel_two, len_x, len_y)
    _, pull_pre = jax.vjp(jax.nn.gelu, pre)
    dpre = pull_pre(dhidden)[0].astype(jnp.bfloat16)
    dpre_rim = with_halo(dpre.reshape(len_x, len_y, NZ * C), (("gx", 0), ("gy", 1)), 1)
    dpre_cycle = dpre_rim.reshape(len_x + 2, len_y + 2, NZ, C)
    dpre_own = dpre_cycle[1:-1, 1:-1]
    grad_two = correlate(padded_h, dtotal, len_x, len_y)
    grad_one = correlate(padded_x, dpre_own, len_x, len_y)
    kernel_one_grad, kernel_two_grad = lax.psum((grad_one, grad_two), ("gx", "gy"))
    dconv = conv_back(pad_depth(dpre_cycle), kernel_one, len_x, len_y)
    dre, dim_part = spectrum_of(dtotal.astype(jnp.float32), tabs)
    spectral_grad, dxre, dxim = weight_grads(
        xre, xim, dre * scale, dim_part * scale, spectral_weight[0], spectral_weight[1]
    )
    field_grad = (
        (dconv + field_of(dxre, dxim, tabs)).astype(jnp.bfloat16).reshape(len_x, len_y, NZ * C)
    )
    return (field_grad, kernel_one_grad, kernel_two_grad, spectral_grad)


def solution(mesh):
    return jax.shard_map(
        shards,
        mesh=mesh,
        in_specs=(
            P("gx", "gy", None),
            P("gx", "gy", None),
            P(),
            P(),
            P(None, ("gx", "gy"), None, None),
        ),
        out_specs=(P("gx", "gy", None), P(), P(), P(None, ("gx", "gy"), None, None)),
        check_vma=False,
    )
```

profile of v0, /device:TPU:32, one launch (start us, length us, event | category | flops | bytes accessed | tf_op | source)
XLA Modules:
  0.0 1794.8 jit_solution(11535673426374168083)
XLA Ops:
  8.0 4.2 collective-permute-start.1
  23.0 3.7 subtract_bitcast_fusion.1
  29.0 5.6 copy.351
  34.5 3.5 reshape.501
  38.1 3.8 copy.348
  41.8 3.5 reshape.500
  49.5 7.8 collective-permute-done.3
  131.8 10.2 reshape.527
  149.6 6.0 collective-permute-start.5
  157.6 5.7 collective-permute-done.4
  163.4 6.9 collective-permute-start.6
  253.0 63.5 %all-reduce.10.cloned.1.call-done = f32[4608,64]{0,1:T(8,128)} async-done(((f32[4608,64]{0,1:T(8,128)}), f32[4608,64]{0,1:T(8,128)}) %all-reduce.10.cloned.1.call-update) | async-done | bytes 1179664
  373.8 365.6 %all-gather.5.cloned.1.call-done = f32[256,18,64]{2,1,0:T(8,128)} async-done(((f32[1,18,64]{2,1,0:T(8,128)}), f32[256,18,64]{2,1,0:T(8,128)}) %all-gather.5.cloned.1.call-update) | async-done | bytes 1179664 | tf_op jit(solution)/shard_map/all_gather | solution.py:170
  739.4 3.9 reshape.630
  743.3 3.1 fusion.794
  768.9 3.5 collective-permute-start.8
  803.9 3.7 fusion.152
  807.6 4.0 subtract_bitcast_fusion
  811.6 5.3 copy.514
  817.0 4.2 reshape.624
  821.1 5.1 add_bitcast_fusion
  826.2 5.3 copy.511
  831.5 4.2 reshape.623
  844.1 4.6 collective-permute-done.11
  852.9 2.9 pad_slice_fusion.18
  968.4 6.0 collective-permute-start.13
  976.5 5.7 collective-permute-done.12
  982.2 6.9 collective-permute-start.14
  995.1 2.7 fusion.795
  1098.3 251.6 %all-reduce.12.cloned.1.call-done = (f32[4608,64]{0,1:T(8,128)}, f32[27,32,32]{2,1,0:T(8,128)}, f32[27,32,32]{2,1,0:T(8,128)}) async-done(((f32[4608,64]{0,1:T(8,128)}, f32[27,32,32]{2,1,0:T(8,128)}, f32[27,32,32]{2,1,0:T(8,128)}), (f32[4608,64]{0,1:T(8,128)}, f32[27,32,32]{2,1,0:T(8,128)}, f32[27,32,32]{2,1,0:T(8,128)})) %all-reduce.12.cloned.1.call-update) | async-done | bytes 1400848
  1370.1 398.1 %all-gather.7.cloned.1.call-done = f32[256,18,64]{2,1,0:T(8,128)} async-done(((f32[1,18,64]{2,1,0:T(8,128)}), f32[256,18,64]{2,1,0:T(8,128)}) %all-gather.7.cloned.1.call-update) | async-done | bytes 1179664 | tf_op jit(solution)/shard_map/all_gather | solution.py:170
  1768.2 2.8 reshape.632
  (698 shorter events, 564.9 us)
Async XLA Ops:
  7.2 309.4 %all-reduce.10.cloned.1.call-start = ((), (), s32[]{:S(2)}) async-start(), calls=%async_computation.2 | async-start | bytes 2359296
  8.0 37.5 %collective-permute-start.1 = (bf16[1,8,1024]{2,1,0:T(8,128)(2,1)S(1)}, bf16[1,8,1024]{2,1,0:T(8,128)(2,1)S(1)}, u32[]{:S(2)}, u32[]{:S(2)}) collective-permute-start(bf16[1,8,1024]{2,1,0:T(8,128)(2,1)S(1)} %get-tuple-element.143), channel_id=1, source_target_pairs={{16,0},{32,16},{48,32},{64,48},{80,64},{96,80},{112,96},{128,112},... | collective-permute-start | bytes 49160 | tf_op jit(solution)/shard_map/ppermute | solution.py:28
  12.2 33.2 %collective-permute-start = (bf16[1,8,1024]{2,1,0:T(8,128)(2,1)S(1)}, bf16[1,8,1024]{2,1,0:T(8,128)(2,1)S(1)}, u32[]{:S(2)}, u32[]{:S(2)}) collective-permute-start(bf16[1,8,1024]{2,1,0:T(8,128)(2,1)S(1)} %get-tuple-element.144), channel_id=1, source_target_pairs={{0,16},{16,32},{32,48},{48,64},{64,80},{80,96},{96,112},{112,128},... | collective-permute-start | bytes 49160 | tf_op jit(solution)/shard_map/ppermute | solution.py:26
  45.5 4.0 collective-permute-start.2
  47.0 10.3 collective-permute-start.3
  49.4 690.0 %all-gather.5.cloned.1.call-start = ((), (), s32[]{:S(2)}) async-start(), calls=%async_computation | async-start | bytes 3158016 | tf_op jit(solution)/shard_map/all_gather | solution.py:170
  147.6 24.6 %copy-start.82 = (bf16[4,8,1024]{2,1,0:T(8,128)(2,1)S(1)}, bf16[4,8,1024]{2,1,0:T(8,128)(2,1)}, u32[]{:S(2)}) copy-start(bf16[4,8,1024]{2,1,0:T(8,128)(2,1)} %param.6) | copy-start | bytes 196612
  149.6 8.0 collective-permute-start.5
  155.6 7.7 collective-permute-start.4
  163.4 9.8 collective-permute-start.6
  170.3 4.0 collective-permute-start.7
  238.2 79.3 %copy-start = (f32[2,18,32,32]{3,2,1,0:T(8,128)S(1)}, f32[2,18,32,32]{3,2,1,0:T(8,128)}, u32[]{:S(2)}) copy-start(f32[2,18,32,32]{3,2,1,0:T(8,128)} %param.9) | copy-start | bytes 442372
  325.7 1024.1 %all-reduce.12.cloned.1.call-start = ((), (), s32[]{:S(2)}) async-start(), calls=%async_computation.3 | async-start | bytes 4128768
  766.6 73.0 %collective-permute-start.9 = (bf16[1,8,1024]{2,0,1:T(2,128)(2,1)}, bf16[1,8,1024]{2,0,1:T(2,128)(2,1)}, u32[]{:S(2)}, u32[]{:S(2)}) collective-permute-start(bf16[1,8,1024]{2,0,1:T(2,128)(2,1)} %slice.924), channel_id=1, source_target_pairs={{16,0},{32,16},{48,32},{64,48},{80,64},{96,80},{112,96},{128,112},... | collective-permute-start | bytes 49160 | tf_op jit(solution)/shard_map/ppermute | solution.py:28
  768.9 70.6 %collective-permute-start.8 = (bf16[1,8,1024]{2,0,1:T(2,128)(2,1)}, bf16[1,8,1024]{2,0,1:T(2,128)(2,1)}, u32[]{:S(2)}, u32[]{:S(2)}) collective-permute-start(bf16[1,8,1024]{2,0,1:T(2,128)(2,1)} %slice.923), channel_id=1, source_target_pairs={{0,16},{16,32},{32,48},{48,64},{64,80},{80,96},{96,112},{112,128},... | collective-permute-start | bytes 49160 | tf_op jit(solution)/shard_map/ppermute | solution.py:26
  778.6 23.1 %copy-start.1 = (f32[4,24,8,32]{3,1,2,0:T(8,128)}, f32[4,24,8,32]{3,1,2,0:T(8,128)S(1)}, u32[]{:S(2)}) copy-start(f32[4,24,8,32]{3,1,2,0:T(8,128)S(1)} %fusion.45) | copy-start | bytes 294916
  840.3 3.8 collective-permute-start.10
  841.6 7.1 collective-permute-start.11
  862.4 20.8 %copy-start.19 = (bf16[27,32,32]{2,1,0:T(8,128)(2,1)S(1)}, bf16[27,32,32]{2,1,0:T(8,128)(2,1)}, u32[]{:S(2)}) copy-start(bf16[27,32,32]{2,1,0:T(8,128)(2,1)} %param.8) | copy-start | bytes 165892
  862.4 21.6 %copy-start.16 = (bf16[4,8,32,32]{3,2,0,1:T(8,128)(2,1)S(1)}, bf16[4,8,32,32]{3,2,0,1:T(8,128)(2,1)}, u32[]{:S(2)}) copy-start(bf16[4,8,32,32]{3,2,0,1:T(8,128)(2,1)} %get-tuple-element.48) | copy-start | bytes 196612
  885.2 20.8 %copy-start.14 = (bf16[4,8,32,32]{3,2,0,1:T(8,128)(2,1)S(1)}, bf16[4,8,32,32]{3,2,0,1:T(8,128)(2,1)}, u32[]{:S(2)}) copy-start(bf16[4,8,32,32]{3,2,0,1:T(8,128)(2,1)} %get-tuple-element.54) | copy-start | bytes 196612
  907.1 21.6 %copy-start.12 = (bf16[4,8,32,32]{3,2,0,1:T(8,128)(2,1)S(1)}, bf16[4,8,32,32]{3,2,0,1:T(8,128)(2,1)}, u32[]{:S(2)}) copy-start(bf16[4,8,32,32]{3,2,0,1:T(8,128)(2,1)} %get-tuple-element.60) | copy-start | bytes 196612
  929.8 21.4 %copy-start.11 = (bf16[4,8,32,32]{3,2,0,1:T(8,128)(2,1)S(1)}, bf16[4,8,32,32]{3,2,0,1:T(8,128)(2,1)}, u32[]{:S(2)}) copy-start(bf16[4,8,32,32]{3,2,0,1:T(8,128)(2,1)} %get-tuple-element.66) | copy-start | bytes 196612
  968.4 8.1 collective-permute-start.13
  974.4 7.7 collective-permute-start.12
  982.2 9.7 collective-permute-start.14
  989.1 4.1 collective-permute-start.15
  1036.2 21.9 %copy-start.13 = (bf16[4,8,32,32]{3,2,0,1:T(8,128)(2,1)S(1)}, bf16[4,8,32,32]{3,2,0,1:T(8,128)(2,1)}, u32[]{:S(2)}) copy-start(bf16[4,8,32,32]{3,2,0,1:T(8,128)(2,1)} %get-tuple-element.38) | copy-start | bytes 196612
  1089.6 260.3 %copy-start.83 = (f32[18]{0:T(128)S(1)}, f32[18]{0:T(128)}, u32[]{:S(2)}) copy-start(f32[18]{0:T(128)} %fusion.532) | copy-start | bytes 220
  1089.6 678.6 %all-gather.7.cloned.1.call-start = ((), (), s32[]{:S(2)}) async-start(), calls=%async_computation.1 | async-start | bytes 3158016 | tf_op jit(solution)/shard_map/all_gather | solution.py:170
  1093.6 261.9 %copy-start.3 = (bf16[4,8,32,32]{3,2,0,1:T(8,128)(2,1)S(1)}, bf16[4,8,32,32]{3,2,0,1:T(8,128)(2,1)}, u32[]{:S(2)}) copy-start(bf16[4,8,32,32]{3,2,0,1:T(8,128)(2,1)} %get-tuple-element.40) | copy-start | bytes 196612
  1095.9 261.0 %copy-start.6 = (bf16[4,8,32,32]{3,2,0,1:T(8,128)(2,1)S(1)}, bf16[4,8,32,32]{3,2,0,1:T(8,128)(2,1)}, u32[]{:S(2)}) copy-start(bf16[4,8,32,32]{3,2,0,1:T(8,128)(2,1)} %get-tuple-element.25) | copy-start | bytes 196612
  (72 other events, 528.1 us)
Sparse Core Ops, SparseCore 0:
  49.5 266.9 all-reduce.9
  325.9 413.5 all-gather.4
  1089.7 260.1 all-reduce.11
  1354.0 414.1 all-gather.6
where the time goes:
time: 1810 us; the launch traced here: 1790 us
  waiting for transfers between devices  1110 us (61%)
  local copies, waits for them, and re-layouts  412 us (23%)
  matrix products  196 us (11%)
  starting transfers between devices  50.9 us (3%)
    all_gather x2, waiting for transfers between devices, field_of(): whole_rows = lax.all_gather(packed, ('gx', 'gy'), axis=0, tiled=True)  764 us
    unnamed x6, waiting for transfers between devices  315 us
    reshape x54, local copies, waits for them, and re-layouts, conv_sum(): padded[a:a + len_x, b:b + len_y, e:e + NZ].reshape(-1, kernel.shape[1])  94.6 us
    slice x57, local copies, waits for them, and re-layouts, conv_back(): padded[2 - a:2 - a + len_x, 2 - b:2 - b + len_y, 2 - e:2 - e + NZ]  92.6 us
    slice x60, local copies, waits for them, and re-layouts, conv_sum(): padded[a:a + len_x, b:b + len_y, e:e + NZ].reshape(-1, kernel.shape[1])  85.6 us
    reshape x53, local copies, waits for them, and re-layouts, conv_back(): padded[2 - a:2 - a + len_x, 2 - b:2 - b + len_y, 2 - e:2 - e + NZ]  69.6 us
    dot_general x54, matrix products, correlate(): jnp.dot(piece.T, flat_grad, preferred_element_type=jnp.float32)  54.3 us
    dot_general x54, matrix products, conv_back(): jnp.dot(piece, kernel[offset].T, preferred_element_type=jnp.float32)  41.1 us
  transfers between devices with their start and end apart: 20, of which 10 were waited for; matrix products, arithmetic and copies ran while one was open for 19% of the time, Pallas kernels for 0%

commit v1 on v0

v1 whole, which is shorter than its diff:
```python
import math

import jax
import jax.numpy as jnp
import numpy as np
from jax import lax
from jax.experimental import pallas as pl
from jax.experimental.pallas import tpu as pltpu
from jax.sharding import PartitionSpec as P

C = 32
MX = 24
MY = 24
MZ = 8
NZ = 32
NX = 64
NY = 128
PEERS = 16
LX = 4
LY = 8
MESH = pl.DeviceIdType.MESH
F32 = jnp.float32
BF16 = jnp.bfloat16
HIGH = lax.Precision.HIGHEST


def kept(length, count):
    half = count // 2
    return np.concatenate([np.arange(half), length - half + np.arange(half)])


def angles(coords, freqs, length):
    return (coords[:, None] * freqs[None, :] % length) * (2.0 * math.pi / length)


def split(table):
    high = table.astype(BF16)
    low = (table - high.astype(np.float64)).astype(BF16)
    return np.stack([high, low])


def constants():
    az = angles(np.arange(NZ), np.arange(MZ), NZ).reshape(NZ, 2, 4)
    fz = np.stack([np.cos(az), -np.sin(az)], axis=2)
    mz = np.einsum("zhrk,ij->zihrkj", fz, np.eye(C)).reshape(NZ * C, 2 * MZ * C)
    ax = angles(np.arange(NX), kept(NX, MX), NX)
    tx = np.stack([np.cos(ax), np.sin(ax)], axis=-1).reshape(PEERS, LX, MX, 2)
    tx = tx.transpose(0, 2, 1, 3).reshape(PEERS, MX * LX * 2)
    ay = angles(np.arange(NY), kept(NY, MY), NY).reshape(PEERS, LY, 4, 6)
    cy = np.zeros((PEERS, 4, 8, LY))
    sy = np.zeros((PEERS, 4, 8, LY))
    cy[:, :, :6] = np.cos(ay).transpose(0, 2, 3, 1)
    sy[:, :, :6] = np.sin(ay).transpose(0, 2, 3, 1)
    cy = cy.reshape(PEERS, 32, LY)
    sy = sy.reshape(PEERS, 32, LY)
    ty = np.concatenate([cy, sy], axis=2)
    tys = ty.transpose(0, 2, 1)
    return (
        split(mz),
        split(mz.T),
        tx.astype(np.float32),
        ty.astype(np.float32),
        tys.astype(np.float32),
    )


def gelu_parts(x):
    k = math.sqrt(2.0 / math.pi)
    t = jnp.tanh(k * (x + 0.044715 * (x * x * x)))
    cdf = 0.5 * (1.0 + t)
    slope = cdf + x * (0.5 * (1.0 - t * t)) * (k * (1.0 + (3.0 * 0.044715) * (x * x)))
    return x * cdf, slope


def dot(a, b, precision=None):
    return jnp.dot(a, b, preferred_element_type=F32, precision=precision)


def body(
    field, cot, kk, sw, mz, mzs, tx, ty, tys,
    out_field, out_kg, out_sg,
    xe, de, xw, hw, dw, pw, pre, brn, band, cg, zt, sp, dts, dtl,
    s1, r1, s2, r2, xt, s3, r3, s4, r4, kgb, r5, s6, r6, s7, r7,
    hs, hr, sx, rx, sy, ry,
):
    gx = lax.axis_index("gx")
    gy = lax.axis_index("gy")

    def around(i, k):
        return lax.rem(i + k + PEERS, PEERS)

    barrier = pltpu.get_barrier_semaphore()

    @pl.loop(1, PEERS)
    def _(k):
        pl.semaphore_signal(barrier, inc=1, device_id=(around(gx, k), gy), device_id_type=MESH)
        pl.semaphore_signal(barrier, inc=1, device_id=(gx, around(gy, k)), device_id_type=MESH)

    for i in (-1, 1):
        for j in (-1, 1):
            pl.semaphore_signal(
                barrier, inc=1, device_id=(around(gx, i), around(gy, j)), device_id_type=MESH
            )

    sides = [(i, j) for i in (-1, 0, 1) for j in (-1, 0, 1) if (i, j) != (0, 0)]
    x_from = {-1: (2, 2), 0: (2, 4), 1: (4, 2)}
    x_to = {-1: (6, 2), 0: (2, 4), 1: (0, 2)}
    y_from = {-1: (1, 1), 0: (1, 4), 1: (4, 1)}
    y_to = {-1: (5, 1), 0: (1, 4), 1: (0, 1)}

    def rim_copy(ext, which, n, i, j):
        return pltpu.make_async_remote_copy(
            src_ref=ext.at[pl.ds(*x_from[i]), pl.ds(*y_from[j])],
            dst_ref=ext.at[pl.ds(*x_to[i]), pl.ds(*y_to[j])],
            send_sem=hs.at[which, n],
            recv_sem=hr.at[which, n],
            device_id=(around(gx, i), around(gy, j)),
            device_id_type=MESH,
        )

    def rim_send(ext, which):
        for n, (i, j) in enumerate(sides):
            rim_copy(ext, which, n, i, j).start()

    def rim_wait(ext, which):
        for n, (i, j) in enumerate(sides):
            rim_copy(ext, which, n, i, j).wait_recv()

    def rim_done(ext, which):
        for n, (i, j) in enumerate(sides):
            rim_copy(ext, which, n, i, j).wait_send()

    def peer_copy(axis, src, src_at, dst, dst_at, send, recv, which, k, peer):
        return pltpu.make_async_remote_copy(
            src_ref=src.at[pl.ds(src_at, 3)],
            dst_ref=dst.at[pl.ds(dst_at, 3)],
            send_sem=send.at[which, k],
            recv_sem=recv.at[which, k],
            device_id=(peer, gy) if axis == "gx" else (gx, peer),
            device_id_type=MESH,
        )

    def exchange(axis, src, dst, which, scatter):
        me = gx if axis == "gx" else gy
        send, recv = (sx, rx) if axis == "gx" else (sy, ry)

        def start(k):
            peer = around(me, k)
            at = 3 * peer if scatter else 0
            peer_copy(axis, src, at, dst, 3 * me, send, recv, which, k, peer).start()

        def arrived(k):
            peer = around(me, -k)
            at = 3 * peer if scatter else 0
            peer_copy(axis, src, at, dst, 3 * peer, send, recv, which, k, peer).wait_recv()

        def done():
            @pl.loop(1, PEERS)
            def _(k):
                peer = around(me, k)
                at = 3 * peer if scatter else 0
                peer_copy(axis, src, at, dst, 3 * me, send, recv, which, k, peer).wait_send()

        return start, arrived, done

    def start_all(start):
        @pl.loop(1, PEERS)
        def _(k):
            start(k)

    def wait_all(arrived):
        @pl.loop(1, PEERS)
        def _(k):
            arrived(k)

    def total_of(dst, shape):
        def add(k, acc):
            return acc + dst[pl.ds(3 * k, 3)].astype(F32)

        return lax.fori_loop(0, PEERS, add, jnp.zeros(shape, F32))

    def z_modes(rows):
        modes = dot(rows, mz[0]) + dot(rows, mz[1])
        for h in range(2):
            zt[h] = modes[:, 256 * h : 256 * h + 256].reshape(LX, LY, 256)

    def x_send(which):
        start, arrived, done = exchange("gx", s1.at[which], r1.at[which], which, True)

        def units(peer):
            for j in range(3):
                unit = 3 * peer + j
                ix = unit // 2
                half = lax.rem(unit, 2)
                re = jnp.zeros((LY, 128), F32)
                im = jnp.zeros((LY, 128), F32)
                for x in range(LX):
                    c = tx[gx, ix * 8 + 2 * x]
                    s = tx[gx, ix * 8 + 2 * x + 1]
                    zr = zt[half, x, :, 0:128]
                    zi = zt[half, x, :, 128:256]
                    re = re + (c * zr + s * zi)
                    im = im + (c * zi - s * zr)
                s1[which, unit] = jnp.concatenate([re, im], axis=0).astype(BF16)

        @pl.loop(1, PEERS)
        def _(k):
            units(around(gx, k))
            start(k)

        units(gx)
        r1[which, pl.ds(3 * gx, 3)] = s1[which, pl.ds(3 * gx, 3)]
        return arrived, done

    lane = lax.broadcasted_iota(jnp.int32, (LY, 128), 1)

    def y_send(which):
        part = total_of(r1.at[which], (3, 16, 128))
        blocks = []
        for u in range(3):
            re = part[u, 0:8]
            im = part[u, 8:16]
            for k in range(4):
                here = (128 - 32 * k) % 128
                after = (160 - 32 * k) % 128
                re_here = pltpu.roll(re, here, 1) if here else re
                im_here = pltpu.roll(im, here, 1) if here else im
                re_after = pltpu.roll(re, after, 1) if after else re
                im_after = pltpu.roll(im, after, 1) if after else im
                straight = jnp.where(lane < 32, re_here, jnp.where(lane < 64, im_after, 0.0))
                crossed = jnp.where(lane < 32, im_here, jnp.where(lane < 64, -re_after, 0.0))
                blocks.append(jnp.concatenate([straight, crossed], axis=0))
        modes = dot(ty[gy], jnp.concatenate(blocks, axis=1), HIGH)
        for p in range(12):
            s2[which, 4 * p : 4 * p + 4] = modes[:, 128 * p : 128 * p + 128].reshape(4, 8, 128)
        start, arrived, done = exchange("gy", s2.at[which], r2.at[which], 2 * which, True)
        start_all(start)
        r2[which, pl.ds(3 * gy, 3)] = s2[which, pl.ds(3 * gy, 3)]
        return arrived, done

    def modes_send(which):
        start, arrived, done = exchange("gy", s3.at[which], r3.at[which], 2 * which + 1, False)
        start_all(start)
        r3[which, pl.ds(3 * gy, 3)] = s3[which]
        return arrived, done

    def columns_send(which):
        blocks = [r3[which, 4 * p : 4 * p + 4].reshape(32, 128) for p in range(12)]
        cells = dot(tys[gy], jnp.concatenate(blocks, axis=1), HIGH)
        for u in range(3):
            re = jnp.zeros((LY, 128), F32)
            im = jnp.zeros((LY, 128), F32)
            for k in range(4):
                at = 128 * (4 * u + k)
                both = cells[0:8, at : at + 128] + pltpu.roll(cells[8:16, at : at + 128], 64, 1)
                mine = lane // 32 == k
                up = 32 * k
                down = (32 * k + 96) % 128
                re = jnp.where(mine, pltpu.roll(both, up, 1) if up else both, re)
                im = jnp.where(mine, pltpu.roll(both, down, 1) if down else both, im)
            s4[which, u] = jnp.concatenate([re, im], axis=0).astype(BF16)
        start, arrived, done = exchange("gx", s4.at[which], r4.at[which], 2 + which, False)
        start_all(start)
        r4[which, pl.ds(3 * gx, 3)] = s4[which]
        return arrived, done

    def cells_of(which):
        def step(jj, acc):
            acc = list(acc)
            for t in range(3):
                ix = 3 * jj + t
                for h in range(2):
                    unit = r4[which, 6 * jj + 2 * t + h].astype(F32)
                    re = unit[0:8]
                    im = unit[8:16]
                    for x in range(LX):
                        c = tx[gx, ix * 8 + 2 * x]
                        s = tx[gx, ix * 8 + 2 * x + 1]
                        at = (h * LX + x) * 2
                        acc[at] = acc[at] + (c * re - s * im)
                        acc[at + 1] = acc[at + 1] + (c * im + s * re)
            return tuple(acc)

        zero = jnp.zeros((LY, 128), F32)
        acc = lax.fori_loop(0, 8, step, (zero,) * 16)
        rows = [
            jnp.concatenate([acc[x * 2], acc[x * 2 + 1], acc[8 + x * 2], acc[9 + x * 2]], axis=1)
            for x in range(LX)
        ]
        modes = jnp.concatenate(rows, axis=0)
        high = modes.astype(BF16)
        low = (modes - high.astype(F32)).astype(BF16)
        return dot(high, mzs[0]) + (dot(high, mzs[1]) + dot(low, mzs[0]))

    def windows(dst, values):
        n = values.shape[0]
        zb = lax.broadcasted_iota(jnp.int32, (n, 8, 128), 1)
        ln = lax.broadcasted_iota(jnp.int32, (n, 8, 128), 2)
        before = pltpu.roll(values, 1, 1)
        after = pltpu.roll(values, 7, 1)
        edge = jnp.where(
            (ln >= 96) & (zb > 0), before, jnp.where((ln < 32) & (zb < 7), after, 0.0)
        )
        dst[:, :, 0:128] = values
        dst[:, :, 128:256] = edge

    def conv(src, kernel, nx, ny, acc):
        acc[...] = jnp.zeros_like(acc)

        @pl.loop(0, 9)
        def _(ab):
            a = ab // 3
            b = lax.rem(ab, 3)
            rows = src[pl.ds(a, nx), pl.ds(b, ny)].reshape(nx * ny * 8, 256).astype(BF16)
            acc[...] += dot(rows, band[kernel, ab])

    def correlate(src, off, grad, q):
        turned = grad.T.astype(BF16)

        @pl.loop(0, 9)
        def _(ab):
            a = ab // 3 + off
            b = lax.rem(ab, 3) + off
            rows = src[pl.ds(a, LX), pl.ds(b, LY)].reshape(256, 256).astype(BF16)
            prod = dot(turned, rows)
            acc = jnp.zeros((C, 256), F32)
            for zl in range(4):
                shift = (32 - 32 * zl) % 256
                piece = prod[32 * zl : 32 * zl + 32]
                acc = acc + (pltpu.roll(piece, shift, 1) if shift else piece)
            tile = acc[:, 0:128].astype(BF16)
            kgb[(q * 9 + ab) * 2] = tile[0:16]
            kgb[(q * 9 + ab) * 2 + 1] = tile[16:32]

    def widen(ext, dst):
        @pl.loop(0, 8)
        def _(i):
            values = ext[i].astype(F32).reshape(12, 8, 128)
            yi = lax.broadcasted_iota(jnp.int32, (12, 8, 128), 0) + (gy * LY - 2)
            row = gx * LX - 2 + i
            ok = (row >= 0) & (row < NX) & (yi >= 0) & (yi < NY)
            windows(dst.at[i], jnp.where(ok, values, 0.0))

    for x in range(LX):
        mine = field[x].astype(F32)
        g = cot[x].astype(F32)
        for b in range(8):
            sp[8 * x : 8 * x + 8, b, :] = mine[:, 128 * b : 128 * b + 128]
            cg[8 * x : 8 * x + 8, b, :] = g[:, 128 * b : 128 * b + 128]
    xe[2:6, 1:5] = sp[...].reshape(4, 4, 16, 128).astype(BF16)
    z_modes(field[...].reshape(32, 1024))

    pl.semaphore_wait(barrier, 2 * (PEERS - 1) + 4)

    rim_send(xe, 0)
    x_arrived, x_done = x_send(0)

    group = lax.broadcasted_iota(jnp.int32, (C, 128), 1) // C
    for q in range(4):

        @pl.loop(0, 9)
        def _(ab):
            taps = [kk[q, 3 * ab + e].astype(F32) for e in range(3)]
            for block in range(8):
                z = block if block < 5 else block - 8
                rows = jnp.zeros((C, 128), F32)
                for e in range(3):
                    if 0 <= z + 1 - e < 4:
                        rows = jnp.where(group == z + 1 - e, taps[e], rows)
                band[q, ab, 32 * block : 32 * block + 32] = rows.astype(BF16)

    kgb[36:48] = jnp.zeros((12, 16, 128), BF16)

    rim_wait(xe, 0)
    widen(xe, xw)
    conv(xw, 0, 6, 10, pre)

    wait_all(x_arrived)
    y_arrived, y_done = y_send(0)

    @pl.loop(0, 6)
    def _(i):
        rows = pl.ds(pl.multiple_of(i * 80, 80), 80)
        h, slope = gelu_parts(pre[rows])
        pre[rows] = slope
        yi = lax.broadcasted_iota(jnp.int32, (10, 8, 128), 0) + (gy * LY - 1)
        row = gx * LX - 1 + i
        ok = (row >= 0) & (row < NX) & (yi >= 0) & (yi < NY)
        h = h.astype(BF16).astype(F32).reshape(10, 8, 128)
        windows(hw.at[i], jnp.where(ok, h, 0.0))

    conv(hw, 1, 4, 8, brn)

    wait_all(y_arrived)
    first = (gx * PEERS + gy) * 18

    def scale_of(m):
        kz = lax.rem((first + m) // MY, MZ)
        return jnp.where(kz == 0, 1.0 / (NX * NY * NZ), 2.0 / (NX * NY * NZ)).astype(F32)

    spectrum = total_of(r2.at[0], (3, 8, 128)).reshape(24, 128)
    xt[...] = jnp.concatenate([spectrum, jnp.zeros((104, 128), F32)], axis=0).T
    s3[...] = jnp.zeros_like(s3)
    for m in range(18):
        j, row = divmod(m, 6)
        at = 8 * j + row
        xr = xt[0:32, at : at + 1]
        xi = xt[32:64, at : at + 1]
        wr = sw[0, m]
        wi = sw[1, m]
        sc = scale_of(m)
        yr = jnp.sum(xr * wr - xi * wi, axis=0, keepdims=True) * sc
        yi = jnp.sum(xr * wi + xi * wr, axis=0, keepdims=True) * sc
        s3[0, j, row : row + 1, :] = jnp.concatenate([yr, yi, -yi, yr], axis=1)
    m_arrived, m_done = modes_send(0)
    wait_all(m_arrived)
    c_arrived, c_done = columns_send(0)
    wait_all(c_arrived)
    spectral = cells_of(0)
    for b in range(8):
        sp[:, b, :] = spectral[:, 128 * b : 128 * b + 128]

    _, slope = gelu_parts(sp[...].reshape(256, 128) + brn[...])
    dtotal = (cg[...].reshape(256, 128) * slope).astype(BF16)
    de[2:6, 1:5] = dtotal.reshape(4, 4, 16, 128)
    rim_send(de, 1)
    dts[...] = dtotal.astype(F32).reshape(32, 8, 128)
    for b in range(8):
        dtl[:, 128 * b : 128 * b + 128] = dts[:, b, :].astype(BF16)
    z_modes(dtl[...])
    x_arrived2, x_done2 = x_send(1)

    correlate(hw, 0, dts[...].reshape(256, 128), 1)
    rim_wait(de, 1)
    widen(de, dw)

    wait_all(x_arrived2)
    y_arrived2, y_done2 = y_send(1)

    conv_ext(dw, 2, pre, pw, band, gx, gy, windows)

    wait_all(y_arrived2)
    grads = total_of(r2.at[1], (3, 8, 128))
    mode_lane = lax.broadcasted_iota(jnp.int32, (128, 128), 1)
    back = jnp.zeros((128, 128), F32)
    for m in range(18):
        j, row = divmod(m, 6)
        at = 8 * j + row
        xr = xt[0:32, at : at + 1]
        xi = xt[32:64, at : at + 1]
        wr = sw[0, m]
        wi = sw[1, m]
        dy = grads[j, row : row + 1, :] * scale_of(m)
        dyr = dy[:, 0:32]
        dyi = dy[:, 32:64]
        out_sg[0, m] = xr * dyr + xi * dyi
        out_sg[1, m] = xr * dyi - xi * dyr
        dxr = jnp.sum(wr * dyr + wi * dyi, axis=1, keepdims=True)
        dxi = jnp.sum(wr * dyi - wi * dyr, axis=1, keepdims=True)
        column = jnp.concatenate([dxr, dxi, -dxi, dxr], axis=0)
        back = jnp.where(mode_lane == at, column, back)
    s3[1] = back.T[0:24].reshape(3, 8, 128)
    m_arrived2, m_done2 = modes_send(1)

    correlate(xw, 1, pw[1:5, 1:9, :, 0:128].reshape(256, 128), 0)
    k_start, k_arrived, k_done = exchange("gx", kgb, r5, 4, True)
    start_all(k_start)
    r5[pl.ds(3 * gx, 3)] = kgb[pl.ds(3 * gx, 3)]

    wait_all(m_arrived2)
    c_arrived2, c_done2 = columns_send(1)

    conv(pw, 3, 4, 8, brn)
    wait_all(k_arrived)
    s6[...] = total_of(r5, (3, 16, 128))
    l_start, l_arrived, l_done = exchange("gy", s6, r6, 4, False)
    start_all(l_start)
    r6[pl.ds(3 * gy, 3)] = s6[...]

    wait_all(c_arrived2)
    spectral = cells_of(1)
    wait_all(l_arrived)
    s7[...] = total_of(r6, (3, 16, 128))
    n_start, n_arrived, n_done = exchange("gx", s7, r7, 5, False)
    start_all(n_start)
    r7[pl.ds(3 * gx, 3)] = s7[...]

    dts[...] = brn[...].reshape(32, 8, 128)
    for b in range(8):
        value = spectral[:, 128 * b : 128 * b + 128] + dts[:, b, :]
        out_field[:, :, 128 * b : 128 * b + 128] = value.reshape(LX, LY, 128).astype(BF16)
    wait_all(n_arrived)
    out_kg[...] = r7[0:36]

    rim_done(xe, 0)
    rim_done(de, 1)
    for done in (
        x_done, y_done, m_done, c_done, x_done2, y_done2, m_done2, c_done2, k_done, l_done, n_done
    ):
        done()


def conv_ext(dw, kernel, slope, pw, band, gx, gy, windows):
    @pl.loop(0, 6)
    def _(i):
        def tap(ab, acc):
            a = ab // 3
            b = lax.rem(ab, 3)
            rows = dw[i + a, pl.ds(b, 10)].reshape(80, 256).astype(BF16)
            return acc + dot(rows, band[kernel, ab])

        dhidden = lax.fori_loop(0, 9, tap, jnp.zeros((80, 128), F32))
        rows = pl.ds(pl.multiple_of(i * 80, 80), 80)
        dpre = (dhidden * slope[rows]).astype(BF16).astype(F32).reshape(10, 8, 128)
        yi = lax.broadcasted_iota(jnp.int32, (10, 8, 128), 0) + (gy * LY - 1)
        row = gx * LX - 1 + i
        ok = (row >= 0) & (row < NX) & (yi >= 0) & (yi < NY)
        windows(pw.at[i], jnp.where(ok, dpre, 0.0))


def shards(field, cotangent, kernel_one, kernel_two, spectral_weight):
    mz, mzs, tx, ty, tys = constants()
    back_two = kernel_two[::-1].transpose(0, 2, 1)
    back_one = kernel_one[::-1].transpose(0, 2, 1)
    kk = jnp.tile(jnp.stack([kernel_one, kernel_two, back_two, back_one]), (1, 1, 1, 4))
    vmem = pl.BlockSpec(memory_space=pltpu.VMEM)
    smem = pl.BlockSpec(memory_space=pltpu.SMEM)

    def buf(shape, dtype=F32):
        return pltpu.VMEM(shape, dtype)

    field_grad, kg, sg = pl.pallas_call(
        body,
        out_shape=(
            jax.ShapeDtypeStruct((LX, LY, NZ * C), BF16),
            jax.ShapeDtypeStruct((36, 16, 128), F32),
            jax.ShapeDtypeStruct(spectral_weight.shape, F32),
        ),
        in_specs=[vmem, vmem, vmem, vmem, vmem, vmem, smem, vmem, vmem],
        out_specs=(vmem, vmem, vmem),
        scratch_shapes=[
            buf((8, 6, 16, 128), BF16),
            buf((8, 6, 16, 128), BF16),
            buf((8, 12, 8, 256)),
            buf((6, 10, 8, 256)),
            buf((8, 12, 8, 256)),
            buf((6, 10, 8, 256)),
            buf((480, 128)),
            buf((256, 128)),
            buf((4, 9, 256, 128), BF16),
            buf((32, 8, 128)),
            buf((2, LX, LY, 256)),
            buf((32, 8, 128)),
            buf((32, 8, 128)),
            buf((32, 1024), BF16),
            buf((2, 48, 16, 128), BF16),
            buf((2, 48, 16, 128), BF16),
            buf((2, 48, 8, 128)),
            buf((2, 48, 8, 128)),
            buf((128, 128)),
            buf((2, 3, 8, 128)),
            buf((2, 48, 8, 128)),
            buf((2, 3, 16, 128), BF16),
            buf((2, 48, 16, 128), BF16),
            buf((48, 16, 128), BF16),
            buf((48, 16, 128), BF16),
            buf((3, 16, 128)),
            buf((48, 16, 128)),
            buf((3, 16, 128)),
            buf((48, 16, 128)),
            pltpu.SemaphoreType.DMA((2, 8)),
            pltpu.SemaphoreType.DMA((2, 8)),
            pltpu.SemaphoreType.DMA((6, PEERS)),
            pltpu.SemaphoreType.DMA((6, PEERS)),
            pltpu.SemaphoreType.DMA((5, PEERS)),
            pltpu.SemaphoreType.DMA((5, PEERS)),
        ],
        compiler_params=pltpu.CompilerParams(
            collective_id=0, has_side_effects=True, vmem_limit_bytes=56 << 20
        ),
    )(field, cotangent, kk, spectral_weight, mz, mzs, tx, ty, tys)
    kg = kg.reshape(2, 9, C, 128)[..., : 3 * C].reshape(2, 9, C, 3, C)
    kg = kg.transpose(0, 1, 3, 4, 2).reshape(2, 27, C, C)
    return (field_grad, kg[0], kg[1], sg)


def solution(mesh):
    return jax.shard_map(
        shards,
        mesh=mesh,
        in_specs=(
            P("gx", "gy", None),
            P("gx", "gy", None),
            P(),
            P(),
            P(None, ("gx", "gy"), None, None),
        ),
        out_specs=(P("gx", "gy", None), P(), P(), P(None, ("gx", "gy"), None, None)),
        check_vma=False,
    )
```

time: 1810 us -> 126 us (0.07)
  waiting for transfers between devices: 1110 us -> 0 us
  local copies, waits for them, and re-layouts: 412 us -> 12.1 us
  matrix products: 196 us -> 0 us
  Pallas kernels: 0 us -> 110 us
  starting transfers between devices: 50.9 us -> 0 us
    all_gather x2 -> x0, waiting for transfers between devices: 764 us -> none  [field_of(): whole_rows = lax.all_gather(packed, ('gx', 'gy'), axis=0, tiled=True)]
    unnamed x6 -> x0, waiting for transfers between devices: 315 us -> none
    dot_general x206 -> x0, matrix products: 196 us -> none  [the longest x54 54.3 us: correlate(): jnp.dot(piece.T, flat_grad, preferred_element_type=jnp.float32)]
    reshape x124 -> x1, local copies, waits for them, and re-layouts: 187 us -> 1.51 us  [shards(): kg = kg.reshape(2, 9, C, 128)[..., :3 * C].reshape(2, 9, C, 3, C)]
    slice x131 -> x3, local copies, waits for them, and re-layouts: 187 us -> 2.2 us  [shards(): return (field_grad, kg[0], kg[1], sg)]
    pallas_call x0 -> x1, Pallas kernels: none -> 110 us  [shards(): pl.pallas_call(body, out_shape=(jax.ShapeDtypeStruct((LX, LY, NZ * C), BF...]
    ppermute x16 -> x0, starting transfers between devices: 50.4 us -> none  [the longest x8 25.8 us: with_halo(): lax.ppermute(tail, axis, [(i, (i + 1) % count) for i in range(ends)])]
    ppermute x16 -> x0, waiting for transfers between devices: 26.3 us -> none  [the longest x8 14.9 us: with_halo(): lax.ppermute(head, axis, [((i + 1) % count, i) for i in range(ends)])]
  transfers between devices with their start and end apart: 20 -> 0, of which waited for: 10 -> 0; matrix products, arithmetic and copies ran while one was open for 19% -> 0% of each run, Pallas kernels for 0% -> 0%
where the time goes in v1:
time: 126 us; the launch traced here: 124 us
  Pallas kernels  110 us (87%)
  local copies, waits for them, and re-layouts  12.1 us (10%)
  other arithmetic  1.28 us (1%)
    pallas_call x1, Pallas kernels, shards(): pl.pallas_call(body, out_shape=(jax.ShapeDtypeStruct((LX, LY, NZ * C), BF...  110 us
    another operation x2, local copies, waits for them, and re-layouts, shards(): jnp.tile(jnp.stack([kernel_one, kernel_two, back_two, back_one]), (1, 1,...  4.74 us
    unnamed x8, local copies, waits for them, and re-layouts  3.63 us

profile of v1, /device:TPU:32, one launch (start us, length us, event | category | flops | bytes accessed | tf_op | source)
XLA Modules:
  0.0 124.4 jit_solution(4460133022757328466)
XLA Ops:
  0.6 1.1 copy.20
  1.7 1.1 copy.19
  2.9 1.3 %pad_maximum_fusion = bf16[4,27,32,32]{3,2,1,0:T(8,128)(2,1)S(1)} fusion(bf16[1,27,32,32]{3,2,1,0:T(8,128)(2,1)S(1)} %get-tuple-element.12, bf16[1,27,32,32]{3,2,1,0:T(8,128)(2,1)S(1)} %get-tuple-element.13, bf16[1,27,32,32]{3,2,1,0:T(8,128)(2,1)} %bitcast.19, bf16[1,27,32,32]{3,2,1,0:T(8,128)(2,1)} %bitcast.18), kind=kLoop, calls=%fused_computation | loop fusion | flops 331776 | bytes 442368 | tf_op jit(solution)/shard_map/stack | solution.py:525
  4.1 2.0 %tile.4 = bf16[4,27,32,4,32]{4,3,2,1,0:T(4,128)(2,1)S(1)} broadcast(bf16[4,27,32,32]{3,2,1,0:T(8,128)(2,1)S(1)} %pad_maximum_fusion), dimensions={0,1,2,4} | broadcast | bytes 1105920 | tf_op jit(solution)/shard_map/tile | solution.py:525
  6.2 2.7 %tile.10.kk = bf16[4,27,32,128]{3,2,1,0:T(8,128)(2,1)} reshape(bf16[4,27,32,4,32]{4,3,2,1,0:T(4,128)(2,1)S(1)} %tile.4) | data formatting | bytes 1769472 | tf_op jit(solution)/shard_map/tile | solution.py:525
  8.9 110.3 %shard_map.129 = (bf16[4,8,1024]{2,1,0:T(8,128)(2,1)}, f32[36,16,128]{2,1,0:T(8,128)}, f32[2,18,32,32]{3,2,1,0:T(8,128)}) custom-call(bf16[4,8,1024]{2,1,0:T(8,128)(2,1)} %field.1, bf16[4,8,1024]{2,1,0:T(8,128)(2,1)} %cot.1, bf16[4,27,32,128]{3,2,1,0:T(8,128)(2,1)} %tile.10.kk, f32[2,18,32,32]{3,2,1,0:T(8,128)} %sw.1, ...), custom_call_target="tpu_custom_call" | custom-call | tf_op jit(solution)/shard_map/pallas_call | solution.py:532
  119.2 1.5 %reshape.24 = f32[2,9,32,3,32]{4,3,2,1,0:T(4,128)S(1)} reshape(f32[2,9,32,96]{3,2,1,0:T(8,128)} %bitcast.22) | data formatting | bytes 442368 | tf_op jit(solution)/shard_map/reshape | solution.py:582
  120.7 0.0 copy-start.1
  120.7 0.0 copy-start
  120.8 0.3 fusion
  121.1 1.0 copy.22
  122.0 1.0 copy.21
  123.0 0.0 copy-done.1
  123.0 0.6 copy.25
  123.6 0.0 copy-done
  123.6 0.8 copy.26
  (1 shorter events, 0.0 us)
Async XLA Ops:
  120.7 2.2 %copy-start.1 = (bf16[4,8,1024]{2,1,0:T(8,128)(2,1)S(1)}, bf16[4,8,1024]{2,1,0:T(8,128)(2,1)}, u32[]{:S(2)}) copy-start(bf16[4,8,1024]{2,1,0:T(8,128)(2,1)} %get-tuple-element.18) | copy-start | bytes 196612
  120.7 2.9 %copy-start = (f32[2,18,32,32]{3,2,1,0:T(8,128)S(1)}, f32[2,18,32,32]{3,2,1,0:T(8,128)}, u32[]{:S(2)}) copy-start(f32[2,18,32,32]{3,2,1,0:T(8,128)} %get-tuple-element.21) | copy-start | bytes 442372

commit v2 on v1

v2 whole, which is shorter than its diff:
```python
import math

import jax
import jax.numpy as jnp
import numpy as np
from jax import lax
from jax.experimental import pallas as pl
from jax.experimental.pallas import tpu as pltpu
from jax.sharding import PartitionSpec as P

C = 32
MX = 24
MY = 24
MZ = 8
NZ = 32
NX = 64
NY = 128
PEERS = 16
LX = 4
LY = 8
MESH = pl.DeviceIdType.MESH
F32 = jnp.float32
BF16 = jnp.bfloat16
HIGH = lax.Precision.HIGHEST


def kept(length, count):
    half = count // 2
    return np.concatenate([np.arange(half), length - half + np.arange(half)])


def angles(coords, freqs, length):
    return (coords[:, None] * freqs[None, :] % length) * (2.0 * math.pi / length)


def split(table):
    high = table.astype(BF16)
    low = (table - high.astype(np.float64)).astype(BF16)
    return np.stack([high, low])


def constants():
    az = angles(np.arange(NZ), np.arange(MZ), NZ).reshape(NZ, 2, 4)
    fz = np.stack([np.cos(az), -np.sin(az)], axis=2)
    mz = np.einsum("zhrk,ij->zihrkj", fz, np.eye(C)).reshape(NZ * C, 2 * MZ * C)
    ax = angles(np.arange(NX), kept(NX, MX), NX)
    tx = np.stack([np.cos(ax), np.sin(ax)], axis=-1).reshape(PEERS, LX, MX, 2)
    tx = tx.transpose(0, 2, 1, 3).reshape(PEERS, MX * LX * 2)
    ay = angles(np.arange(NY), kept(NY, MY), NY).reshape(PEERS, LY, 12, 2)
    cy = np.zeros((PEERS, 2, 16, LY))
    sy = np.zeros((PEERS, 2, 16, LY))
    cy[:, :, :12] = np.cos(ay).transpose(0, 3, 2, 1)
    sy[:, :, :12] = np.sin(ay).transpose(0, 3, 2, 1)
    ty = np.concatenate([cy, sy], axis=3).reshape(PEERS, 32, 16)
    tys = np.stack([cy, sy], axis=1).transpose(0, 1, 2, 4, 3).reshape(PEERS, 32, 16)
    return (
        split(mz),
        split(mz.T),
        tx.astype(np.float32),
        ty.astype(np.float32),
        tys.astype(np.float32),
    )


def gelu_parts(x):
    k = math.sqrt(2.0 / math.pi)
    t = jnp.tanh(k * (x + 0.044715 * (x * x * x)))
    cdf = 0.5 * (1.0 + t)
    slope = cdf + x * (0.5 * (1.0 - t * t)) * (k * (1.0 + (3.0 * 0.044715) * (x * x)))
    return x * cdf, slope


def dot(a, b, precision=None):
    return jnp.dot(a, b, preferred_element_type=F32, precision=precision)


def body(
    field, cot, k1, k2, sw_hbm, mz_hbm, mzs_hbm, tx, ty, tys,
    out_field, out_k1, out_k2, out_sg,
    sw, mz, mzs, taps, wide,
    xe, de, xw, hw, dw, pw, pre, brn, band, cg, zt, sp, dts, dtl,
    s1, r1, s2, r2, xs, xt, yf, yg, s3, r3, s4, r4, kgf, kgb, r5, s6, r6, s7, r7,
    hs, hr, sx, rx, sy, ry, ls,
):
    load_z = pltpu.make_async_copy(mz_hbm, mz, ls.at[0])
    load_w = pltpu.make_async_copy(sw_hbm, sw, ls.at[1])
    load_zs = pltpu.make_async_copy(mzs_hbm, mzs, ls.at[2])
    load_z.start()
    load_w.start()
    load_zs.start()
    gx = lax.axis_index("gx")
    gy = lax.axis_index("gy")

    def around(i, k):
        return lax.rem(i + k + PEERS, PEERS)

    barrier = pltpu.get_barrier_semaphore()

    @pl.loop(1, PEERS)
    def _(k):
        pl.semaphore_signal(barrier, inc=1, device_id=(around(gx, k), gy), device_id_type=MESH)
        pl.semaphore_signal(barrier, inc=1, device_id=(gx, around(gy, k)), device_id_type=MESH)

    for i in (-1, 1):
        for j in (-1, 1):
            pl.semaphore_signal(
                barrier, inc=1, device_id=(around(gx, i), around(gy, j)), device_id_type=MESH
            )

    sides = [(i, j) for i in (-1, 0, 1) for j in (-1, 0, 1) if (i, j) != (0, 0)]
    x_from = {-1: (2, 2), 0: (2, 4), 1: (4, 2)}
    x_to = {-1: (6, 2), 0: (2, 4), 1: (0, 2)}
    y_from = {-1: (1, 1), 0: (1, 4), 1: (4, 1)}
    y_to = {-1: (5, 1), 0: (1, 4), 1: (0, 1)}

    def rim_copy(ext, which, n, i, j):
        return pltpu.make_async_remote_copy(
            src_ref=ext.at[pl.ds(*x_from[i]), pl.ds(*y_from[j])],
            dst_ref=ext.at[pl.ds(*x_to[i]), pl.ds(*y_to[j])],
            send_sem=hs.at[which, n],
            recv_sem=hr.at[which, n],
            device_id=(around(gx, i), around(gy, j)),
            device_id_type=MESH,
        )

    def rim_send(ext, which):
        for n, (i, j) in enumerate(sides):
            rim_copy(ext, which, n, i, j).start()

    def rim_wait(ext, which):
        for n, (i, j) in enumerate(sides):
            rim_copy(ext, which, n, i, j).wait_recv()

    def rim_done(ext, which):
        for n, (i, j) in enumerate(sides):
            rim_copy(ext, which, n, i, j).wait_send()

    def exchange(axis, src, dst, which, scatter, n):
        me = gx if axis == "gx" else gy
        send, recv = (sx, rx) if axis == "gx" else (sy, ry)

        def copy(k, peer, slot):
            return pltpu.make_async_remote_copy(
                src_ref=src.at[pl.ds(n * peer if scatter else 0, n)],
                dst_ref=dst.at[pl.ds(n * slot, n)],
                send_sem=send.at[which, k],
                recv_sem=recv.at[which, k],
                device_id=(peer, gy) if axis == "gx" else (gx, peer),
                device_id_type=MESH,
            )

        def start(k):
            copy(k, around(me, k), me).start()

        def arrived(k):
            peer = around(me, -k)
            copy(k, peer, peer).wait_recv()

        def done():
            @pl.loop(1, PEERS)
            def _(k):
                copy(k, around(me, k), me).wait_send()

        return start, arrived, done

    def start_all(start):
        @pl.loop(1, PEERS)
        def _(k):
            start(k)

    def wait_all(arrived):
        @pl.loop(1, PEERS)
        def _(k):
            arrived(k)

    def total_of(dst, n):
        def add(k, acc):
            return acc + dst[pl.ds(n * k, n)].astype(F32)

        return lax.fori_loop(0, PEERS, add, jnp.zeros((n,) + dst.shape[1:], F32))

    def z_modes(rows):
        modes = dot(rows, mz[0]) + dot(rows, mz[1])
        for h in range(2):
            zt[h] = modes[:, 256 * h : 256 * h + 256].reshape(LX, LY, 256)

    def x_send(which):
        start, arrived, done = exchange("gx", s1.at[which], r1.at[which], which, True, 3)

        def units(peer):
            for j in range(3):
                unit = 3 * peer + j
                ix = unit // 2
                half = lax.rem(unit, 2)
                re = jnp.zeros((LY, 128), F32)
                im = jnp.zeros((LY, 128), F32)
                for x in range(LX):
                    c = tx[gx, ix * 8 + 2 * x]
                    s = tx[gx, ix * 8 + 2 * x + 1]
                    zr = zt[half, x, :, 0:128]
                    zi = zt[half, x, :, 128:256]
                    re = re + (c * zr + s * zi)
                    im = im + (c * zi - s * zr)
                s1[which, unit] = jnp.concatenate([re, im], axis=0).astype(BF16)

        @pl.loop(1, PEERS)
        def _(k):
            units(around(gx, k))
            start(k)

        units(gx)
        r1[which, pl.ds(3 * gx, 3)] = s1[which, pl.ds(3 * gx, 3)]
        return arrived, done

    lane = lax.broadcasted_iota(jnp.int32, (LY, 128), 1)

    def y_send(which):
        part = total_of(r1.at[which], 3)
        blocks = []
        for u in range(3):
            re = part[u, 0:8]
            im = part[u, 8:16]
            for k in range(4):
                here = (128 - 32 * k) % 128
                after = (160 - 32 * k) % 128
                re_here = pltpu.roll(re, here, 1) if here else re
                im_here = pltpu.roll(im, here, 1) if here else im
                re_after = pltpu.roll(re, after, 1) if after else re
                im_after = pltpu.roll(im, after, 1) if after else im
                straight = jnp.where(lane < 32, re_here, jnp.where(lane < 64, im_after, 0.0))
                crossed = jnp.where(lane < 32, im_here, jnp.where(lane < 64, -re_after, 0.0))
                blocks.append(jnp.concatenate([straight, crossed], axis=0))
        modes = dot(ty[gy], jnp.concatenate(blocks, axis=1), HIGH)
        for p in range(12):
            at = 128 * p
            rows = modes[0:16, at : at + 128] + pltpu.roll(modes[16:32, at : at + 128], 64, 1)
            yf[12 * p : 12 * p + 12] = rows[0:12]
        for d in range(PEERS):
            s2[which, d] = yf[9 * d : 9 * d + 9]
        start, arrived, done = exchange("gy", s2.at[which], r2.at[which], 2 * which, True, 1)
        start_all(start)
        r2[which, gy] = s2[which, gy]
        return arrived, done

    def modes_send(which):
        start, arrived, done = exchange("gy", s3.at[which], r3.at[which], 2 * which + 1, False, 1)
        start_all(start)
        r3[which, gy] = s3[which, 0]
        return arrived, done

    def columns_send(which):
        for d in range(PEERS):
            row = 9 * d
            while row < 9 * d + 9:
                p = row // 12
                end = min(9 * d + 9, 12 * p + 12)
                yg[p, row - 12 * p : end - 12 * p] = r3[which, d, row - 9 * d : end - 9 * d]
                row = end
        cells = dot(tys[gy], jnp.concatenate([yg[p] for p in range(12)], axis=1), HIGH)
        for u in range(3):
            re = jnp.zeros((LY, 128), F32)
            im = jnp.zeros((LY, 128), F32)
            for k in range(4):
                at = 128 * (4 * u + k)
                cell = cells[:, at : at + 128]
                cosine = cell[0:8] + pltpu.roll(cell[8:16], 64, 1)
                sine = cell[16:24] + pltpu.roll(cell[24:32], 64, 1)
                both = cosine + jnp.where(
                    lane < 32, -pltpu.roll(sine, 96, 1), pltpu.roll(sine, 32, 1)
                )
                mine = lane // 32 == k
                up = 32 * k
                down = (32 * k + 96) % 128
                re = jnp.where(mine, pltpu.roll(both, up, 1) if up else both, re)
                im = jnp.where(mine, pltpu.roll(both, down, 1) if down else both, im)
            s4[which, u] = jnp.concatenate([re, im], axis=0).astype(BF16)
        start, arrived, done = exchange("gx", s4.at[which], r4.at[which], 2 + which, False, 3)
        start_all(start)
        r4[which, pl.ds(3 * gx, 3)] = s4[which]
        return arrived, done

    def cells_of(which):
        def step(jj, acc):
            acc = list(acc)
            for t in range(3):
                ix = 3 * jj + t
                for h in range(2):
                    unit = r4[which, 6 * jj + 2 * t + h].astype(F32)
                    re = unit[0:8]
                    im = unit[8:16]
                    for x in range(LX):
                        c = tx[gx, ix * 8 + 2 * x]
                        s = tx[gx, ix * 8 + 2 * x + 1]
                        at = (h * LX + x) * 2
                        acc[at] = acc[at] + (c * re - s * im)
                        acc[at + 1] = acc[at + 1] + (c * im + s * re)
            return tuple(acc)

        zero = jnp.zeros((LY, 128), F32)
        acc = lax.fori_loop(0, 8, step, (zero,) * 16)
        rows = [
            jnp.concatenate([acc[x * 2], acc[x * 2 + 1], acc[8 + x * 2], acc[9 + x * 2]], axis=1)
            for x in range(LX)
        ]
        modes = jnp.concatenate(rows, axis=0)
        high = modes.astype(BF16)
        low = (modes - high.astype(F32)).astype(BF16)
        return dot(high, mzs[0]) + (dot(high, mzs[1]) + dot(low, mzs[0]))

    def windows(dst, i, values):
        n = values.shape[0]
        zb = lax.broadcasted_iota(jnp.int32, (n, 8, 128), 1)
        ln = lax.broadcasted_iota(jnp.int32, (n, 8, 128), 2)
        before = pltpu.roll(values, 1, 1)
        after = pltpu.roll(values, 7, 1)
        edge = jnp.where(
            (ln >= 96) & (zb > 0), before, jnp.where((ln < 32) & (zb < 7), after, 0.0)
        )
        for part, lanes in ((values, 0), (edge, 128)):
            even = part.reshape(n // 2, 16, 128).astype(BF16)
            odd = part[1 : n - 1].reshape(n // 2 - 1, 16, 128).astype(BF16)
            dst[0, i, :, :, lanes : lanes + 128] = even
            dst[1, i, 0 : n // 2 - 1, :, lanes : lanes + 128] = odd

    def conv(src, kernel, nx, ny, acc):
        total = jnp.zeros((nx * ny * 8, 128), F32)
        for ab in range(9):
            a, b = divmod(ab, 3)
            rows = src[b % 2, a : a + nx, b // 2 : b // 2 + ny // 2].reshape(nx * ny * 8, 256)
            total = total + dot(rows, band[kernel, ab])
        acc[...] = total

    def correlate(src, off, grad, q):
        turned = grad.T.astype(BF16)

        lanes = lax.broadcasted_iota(jnp.int32, (C, 256), 1)
        for ab in range(9):
            a, b = divmod(ab, 3)
            a, b = a + off, b + off
            rows = src[b % 2, a : a + LX, b // 2 : b // 2 + LY // 2].reshape(256, 256)
            prod = dot(turned, rows)
            group, place = divmod((q * 9 + ab) * 3, 4)
            first_lane = 32 * place
            acc = jnp.zeros((C, 256), F32)
            for zl in range(4):
                shift = (32 - 32 * zl + first_lane) % 256
                piece = prod[32 * zl : 32 * zl + 32]
                acc = acc + (pltpu.roll(piece, shift, 1) if shift else piece)
            acc = jnp.where((lanes >= first_lane) & (lanes < first_lane + 96), acc, 0.0)
            kgf[32 * group : 32 * group + 32] += acc[:, 0:128]
            if first_lane + 96 > 128:
                kgf[32 * group + 32 : 32 * group + 64] += acc[:, 128:256]

    def widen(ext, dst):
        @pl.loop(0, 8)
        def _(i):
            values = ext[i].astype(F32).reshape(12, 8, 128)
            yi = lax.broadcasted_iota(jnp.int32, (12, 8, 128), 0) + (gy * LY - 2)
            row = gx * LX - 2 + i
            ok = (row >= 0) & (row < NX) & (yi >= 0) & (yi < NY)
            windows(dst, i, jnp.where(ok, values, 0.0))

    for x in range(LX):
        mine = field[x].astype(F32)
        g = cot[x].astype(F32)
        for b in range(8):
            sp[8 * x : 8 * x + 8, b, :] = mine[:, 128 * b : 128 * b + 128]
            cg[8 * x : 8 * x + 8, b, :] = g[:, 128 * b : 128 * b + 128]
    xe[2:6, 1:5] = sp[...].reshape(4, 4, 16, 128).astype(BF16)
    load_z.wait()
    z_modes(field[...].reshape(32, 1024))

    pl.semaphore_wait(barrier, 2 * (PEERS - 1) + 4)

    x_arrived, x_done = x_send(0)
    rim_send(xe, 0)

    group = lax.broadcasted_iota(jnp.int32, (C, 128), 1) // C
    for q, kernel in ((0, k1), (1, k2)):

        @pl.loop(0, 9)
        def _(ab):
            wide = []
            for e in range(3):
                tap = kernel[3 * ab + e].astype(F32)
                wide.append(jnp.concatenate([tap] * 4, axis=1))
            for block in range(8):
                z = block if block < 5 else block - 8
                rows = jnp.zeros((C, 128), F32)
                for e in range(3):
                    if 0 <= z + 1 - e < 4:
                        rows = jnp.where(group == z + 1 - e, wide[e], rows)
                taps[32 * block : 32 * block + 32] = rows
            band[q, ab] = taps[...].astype(BF16)
            band[3 - q, 8 - ab, 0:128] = taps[0:128].T.astype(BF16)
            band[3 - q, 8 - ab, 128:256] = taps[128:256].T.astype(BF16)

    kgf[...] = jnp.zeros_like(kgf)
    yg[...] = jnp.zeros_like(yg)

    rim_wait(xe, 0)
    widen(xe, xw)
    conv(xw, 0, 6, 10, pre)

    wait_all(x_arrived)
    y_arrived, y_done = y_send(0)

    @pl.loop(0, 6)
    def _(i):
        rows = pl.ds(pl.multiple_of(i * 80, 80), 80)
        h, slope = gelu_parts(pre[rows])
        pre[rows] = slope
        yi = lax.broadcasted_iota(jnp.int32, (10, 8, 128), 0) + (gy * LY - 1)
        row = gx * LX - 1 + i
        ok = (row >= 0) & (row < NX) & (yi >= 0) & (yi < NY)
        h = h.astype(BF16).astype(F32).reshape(10, 8, 128)
        windows(hw, i, jnp.where(ok, h, 0.0))

    conv(hw, 1, 4, 8, brn)

    wait_all(y_arrived)
    load_w.wait()
    first = (gx * PEERS + gy) * 18

    def scale_of(m):
        kz = lax.rem((first + m) // MY, MZ)
        return jnp.where(kz == 0, 1.0 / (NX * NY * NZ), 2.0 / (NX * NY * NZ)).astype(F32)

    xs[...] = jnp.zeros_like(xs)
    xs[0:9] = total_of(r2.at[0], 1)[0]
    xt[...] = xs[...].T
    for t in range(9):
        row = []
        for half in range(2):
            m = 2 * t + half
            xr = xt[64 * half : 64 * half + 32, t : t + 1]
            xi = xt[64 * half + 32 : 64 * half + 64, t : t + 1]
            wr = sw[0, m]
            wi = sw[1, m]
            row.append(jnp.sum(xr * wr - xi * wi, axis=0, keepdims=True) * scale_of(m))
            row.append(jnp.sum(xr * wi + xi * wr, axis=0, keepdims=True) * scale_of(m))
        s3[0, 0, t : t + 1, :] = jnp.concatenate(row, axis=1)
    m_arrived, m_done = modes_send(0)
    wait_all(m_arrived)
    c_arrived, c_done = columns_send(0)
    load_zs.wait()
    wait_all(c_arrived)
    spectral = cells_of(0)
    for b in range(8):
        sp[:, b, :] = spectral[:, 128 * b : 128 * b + 128]

    _, slope = gelu_parts(sp[...].reshape(256, 128) + brn[...])
    dtotal = (cg[...].reshape(256, 128) * slope).astype(BF16)
    de[2:6, 1:5] = dtotal.reshape(4, 4, 16, 128)
    rim_send(de, 1)
    dts[...] = dtotal.astype(F32).reshape(32, 8, 128)
    for b in range(8):
        dtl[:, 128 * b : 128 * b + 128] = dts[:, b, :].astype(BF16)
    z_modes(dtl[...])
    x_arrived2, x_done2 = x_send(1)

    rim_wait(de, 1)
    widen(de, dw)
    conv(dw, 2, 6, 10, wide)

    @pl.loop(0, 6)
    def _(i):
        rows = pl.ds(pl.multiple_of(i * 80, 80), 80)
        dpre = (wide[rows] * pre[rows]).astype(BF16).astype(F32).reshape(10, 8, 128)
        yi = lax.broadcasted_iota(jnp.int32, (10, 8, 128), 0) + (gy * LY - 1)
        row = gx * LX - 1 + i
        ok = (row >= 0) & (row < NX) & (yi >= 0) & (yi < NY)
        windows(pw, i, jnp.where(ok, dpre, 0.0))

    wait_all(x_arrived2)
    y_arrived2, y_done2 = y_send(1)

    correlate(hw, 0, dts[...].reshape(256, 128), 1)
    correlate(xw, 1, pw[1, 1:5, 0:4, :, 0:128].reshape(256, 128).astype(F32), 0)
    for d in range(PEERS):
        kgb[d] = kgf[28 * d : 28 * d + 32].astype(BF16)
    k_start, k_arrived, k_done = exchange("gx", kgb, r5, 4, True, 1)
    start_all(k_start)
    r5[gx] = kgb[gx]

    wait_all(y_arrived2)
    xs[0:9] = total_of(r2.at[1], 1)[0]
    mode_lane = lax.broadcasted_iota(jnp.int32, (128, 128), 1)
    back = jnp.zeros((128, 128), F32)
    for t in range(9):
        column = []
        for half in range(2):
            m = 2 * t + half
            xr = xt[64 * half : 64 * half + 32, t : t + 1]
            xi = xt[64 * half + 32 : 64 * half + 64, t : t + 1]
            wr = sw[0, m]
            wi = sw[1, m]
            dy = xs[t : t + 1, :] * scale_of(m)
            dyr = dy[:, 64 * half : 64 * half + 32]
            dyi = dy[:, 64 * half + 32 : 64 * half + 64]
            out_sg[0, m] = xr * dyr + xi * dyi
            out_sg[1, m] = xr * dyi - xi * dyr
            column.append(jnp.sum(wr * dyr + wi * dyi, axis=1, keepdims=True))
            column.append(jnp.sum(wr * dyi - wi * dyr, axis=1, keepdims=True))
        back = jnp.where(mode_lane == t, jnp.concatenate(column, axis=0), back)
    xs[...] = back.T
    s3[1, 0] = xs[0:9]
    m_arrived2, m_done2 = modes_send(1)

    wait_all(k_arrived)
    s6[0] = total_of(r5, 1)[0, 0:28]
    l_start, l_arrived, l_done = exchange("gy", s6, r6, 4, False, 1)
    start_all(l_start)
    r6[gy] = s6[0]
    conv(pw, 3, 4, 8, brn)

    wait_all(m_arrived2)
    c_arrived2, c_done2 = columns_send(1)

    wait_all(l_arrived)
    s7[...] = total_of(r6, 1)
    n_start, n_arrived, n_done = exchange("gx", s7, r7, 5, False, 1)
    start_all(n_start)
    r7[gx] = s7[0]

    wait_all(c_arrived2)
    spectral = cells_of(1)
    dts[...] = brn[...].reshape(32, 8, 128)
    for b in range(8):
        value = spectral[:, 128 * b : 128 * b + 128] + dts[:, b, :]
        out_field[:, :, 128 * b : 128 * b + 128] = value.reshape(LX, LY, 128).astype(BF16)
    wait_all(n_arrived)
    for d in range(PEERS):
        kgf[28 * d : 28 * d + 28] = r7[d]
    for group in range(14):
        turned = kgf[32 * group : 32 * group + 32].T
        for place in range(4):
            block = 4 * group + place
            if block < 54:
                out = out_k1 if block < 27 else out_k2
                out[block % 27] = turned[32 * place : 32 * place + 32]

    rim_done(xe, 0)
    rim_done(de, 1)
    for done in (
        x_done, y_done, m_done, c_done, x_done2, y_done2, m_done2, c_done2, k_done, l_done, n_done
    ):
        done()


def hand_over(*refs):
    for source, target in zip(refs[:4], refs[4:]):
        target[...] = source[...]


def shards(field, cotangent, kernel_one, kernel_two, spectral_weight):
    mz, mzs, tx, ty, tys = constants()
    vmem = pl.BlockSpec(memory_space=pltpu.VMEM)
    hbm = pl.BlockSpec(memory_space=pl.ANY)
    smem = pl.BlockSpec(memory_space=pltpu.SMEM)

    def buf(shape, dtype=F32):
        return pltpu.VMEM(shape, dtype)

    results = pl.pallas_call(
        body,
        out_shape=(
            jax.ShapeDtypeStruct((LX, LY, NZ * C), BF16),
            jax.ShapeDtypeStruct((27, C, C), F32),
            jax.ShapeDtypeStruct((27, C, C), F32),
            jax.ShapeDtypeStruct(spectral_weight.shape, F32),
        ),
        in_specs=[vmem, vmem, vmem, vmem, hbm, hbm, hbm, smem, vmem, vmem],
        out_specs=(vmem, vmem, vmem, vmem),
        scratch_shapes=[
            buf(spectral_weight.shape),
            buf(mz.shape, BF16),
            buf(mzs.shape, BF16),
            buf((256, 128)),
            buf((480, 128)),
            buf((8, 6, 16, 128), BF16),
            buf((8, 6, 16, 128), BF16),
            buf((2, 8, 6, 16, 256), BF16),
            buf((2, 6, 5, 16, 256), BF16),
            buf((2, 8, 6, 16, 256), BF16),
            buf((2, 6, 5, 16, 256), BF16),
            buf((480, 128)),
            buf((256, 128)),
            buf((4, 9, 256, 128), BF16),
            buf((32, 8, 128)),
            buf((2, LX, LY, 256)),
            buf((32, 8, 128)),
            buf((32, 8, 128)),
            buf((32, 1024), BF16),
            buf((2, 48, 16, 128), BF16),
            buf((2, 48, 16, 128), BF16),
            buf((2, PEERS, 9, 128)),
            buf((2, PEERS, 9, 128)),
            buf((128, 128)),
            buf((128, 128)),
            buf((144, 128)),
            buf((12, 16, 128)),
            buf((2, 1, 9, 128)),
            buf((2, PEERS, 9, 128)),
            buf((2, 3, 16, 128), BF16),
            buf((2, 48, 16, 128), BF16),
            buf((480, 128)),
            buf((PEERS, 32, 128), BF16),
            buf((PEERS, 32, 128), BF16),
            buf((1, 28, 128)),
            buf((PEERS, 28, 128)),
            buf((1, 28, 128)),
            buf((PEERS, 28, 128)),
            pltpu.SemaphoreType.DMA((2, 8)),
            pltpu.SemaphoreType.DMA((2, 8)),
            pltpu.SemaphoreType.DMA((6, PEERS)),
            pltpu.SemaphoreType.DMA((6, PEERS)),
            pltpu.SemaphoreType.DMA((5, PEERS)),
            pltpu.SemaphoreType.DMA((5, PEERS)),
            pltpu.SemaphoreType.DMA((3,)),
        ],
        compiler_params=pltpu.CompilerParams(
            collective_id=0, has_side_effects=True, vmem_limit_bytes=56 << 20
        ),
    )(field, cotangent, kernel_one, kernel_two, spectral_weight, mz, mzs, tx, ty, tys)
    return pl.pallas_call(
        hand_over,
        out_shape=tuple(jax.ShapeDtypeStruct(r.shape, r.dtype) for r in results),
        in_specs=[vmem] * 4,
        out_specs=(vmem,) * 4,
    )(*results)


def solution(mesh):
    return jax.shard_map(
        shards,
        mesh=mesh,
        in_specs=(
            P("gx", "gy", None),
            P("gx", "gy", None),
            P(),
            P(),
            P(None, ("gx", "gy"), None, None),
        ),
        out_specs=(P("gx", "gy", None), P(), P(), P(None, ("gx", "gy"), None, None)),
        check_vma=False,
    )
```

time: 126 us -> 95.8 us (0.76)
  Pallas kernels: 110 us -> 93.9 us
  local copies, waits for them, and re-layouts: 12.1 us -> 0 us
  other arithmetic: 1.28 us -> 0 us
    pallas_call x1, Pallas kernels: 110 us -> 91.4 us  [shards(): pl.pallas_call(body, out_shape=(jax.ShapeDtypeStruct((LX, LY, NZ * C), BF...]
    another operation x3 -> x0, local copies, waits for them, and re-layouts: 4.78 us -> none  [the longest x2 4.74 us: shards(): jnp.tile(jnp.stack([kernel_one, kernel_two, back_two, back_one]), (1, 1,...]
    unnamed x8 -> x0, local copies, waits for them, and re-layouts: 3.63 us -> none
    pallas_call x0 -> x1, Pallas kernels: none -> 2.52 us  [shards(): pl.pallas_call(hand_over, out_shape=tuple((jax.ShapeDtypeStruct(r.shape,...]
    slice x3 -> x0, local copies, waits for them, and re-layouts: 2.2 us -> none  [shards(): return (field_grad, kg[0], kg[1], sg)]
    reshape x1 -> x0, local copies, waits for them, and re-layouts: 1.51 us -> none  [shards(): kg = kg.reshape(2, 9, C, 128)[..., :3 * C].reshape(2, 9, C, 3, C)]
    another operation x1 -> x0, other arithmetic: 1.28 us -> none  [shards(): jnp.stack([kernel_one, kernel_two, back_two, back_one])]
where the time goes in v2:
time: 95.8 us; the launch traced here: 94.6 us
  Pallas kernels  93.9 us (98%)
    pallas_call x1, Pallas kernels, shards(): pl.pallas_call(body, out_shape=(jax.ShapeDtypeStruct((LX, LY, NZ * C), BF...  91.4 us
    pallas_call x1, Pallas kernels, shards(): pl.pallas_call(hand_over, out_shape=tuple((jax.ShapeDtypeStruct(r.shape,...  2.52 us

profile of v2, /device:TPU:32, one launch (start us, length us, event | category | flops | bytes accessed | tf_op | source)
XLA Modules:
  0.0 94.6 jit_solution(6021606592279189746)
XLA Ops:
  0.6 91.4 %shard_map.129 = (bf16[4,8,1024]{2,1,0:T(8,128)(2,1)}, f32[27,32,32]{2,1,0:T(8,128)}, f32[27,32,32]{2,1,0:T(8,128)}, f32[2,18,32,32]{3,2,1,0:T(8,128)}) custom-call(bf16[4,8,1024]{2,1,0:T(8,128)(2,1)} %field.1, bf16[4,8,1024]{2,1,0:T(8,128)(2,1)} %cot.1, bf16[27,32,32]{2,1,0:T(8,128)(2,1)} %k1.1, bf16[27,32,32]{2,1,0:T(8,128)(2,1)} %k2.1, ...), custom_call_target="tpu_custom_call" | custom-call | tf_op jit(solution)/shard_map/pallas_call | solution.py:565
  92.0 2.5 %shard_map.130 = (bf16[4,8,1024]{2,1,0:T(8,128)(2,1)}, f32[27,32,32]{2,1,0:T(8,128)}, f32[27,32,32]{2,1,0:T(8,128)}, f32[2,18,32,32]{3,2,1,0:T(8,128)}) custom-call(bf16[4,8,1024]{2,1,0:T(8,128)(2,1)} %get-tuple-element.8.refs_0_, f32[27,32,32]{2,1,0:T(8,128)} %get-tuple-element.9.refs_1_, f32[27,32,32]{2,1,0:T(8,128)} %get-tuple-element.10.refs_2_, ...), custom_call_target="tpu_custom_call" | custom-call | tf_op jit(solution)/shard_map/pallas_call | solution.py:626

commit v3 on v2

--- a/solution.py
+++ b/solution.py
@@ -42,7 +42,9 @@
 def constants():
     az = angles(np.arange(NZ), np.arange(MZ), NZ).reshape(NZ, 2, 4)
     fz = np.stack([np.cos(az), -np.sin(az)], axis=2)
-    mz = np.einsum("zhrk,ij->zihrkj", fz, np.eye(C)).reshape(NZ * C, 2 * MZ * C)
+    fz = fz.reshape(NZ, 2 * MZ)
+    mz = np.repeat(fz, C, axis=1)
+    mzs = np.repeat(fz.T, C, axis=1)
     ax = angles(np.arange(NX), kept(NX, MX), NX)
     tx = np.stack([np.cos(ax), np.sin(ax)], axis=-1).reshape(PEERS, LX, MX, 2)
     tx = tx.transpose(0, 2, 1, 3).reshape(PEERS, MX * LX * 2)
@@ -54,8 +56,8 @@
     ty = np.concatenate([cy, sy], axis=3).reshape(PEERS, 32, 16)
     tys = np.stack([cy, sy], axis=1).transpose(0, 1, 2, 4, 3).reshape(PEERS, 32, 16)
     return (
-        split(mz),
-        split(mz.T),
+        split(mz).astype(np.float32),
+        split(mzs).astype(np.float32),
         tx.astype(np.float32),
         ty.astype(np.float32),
         tys.astype(np.float32),
@@ -75,21 +77,27 @@
 
 
 def body(
-    field, cot, k1, k2, sw_hbm, mz_hbm, mzs_hbm, tx, ty, tys,
+    field, cot, k1_hbm, k2_hbm, sw_hbm, fz, fzs, tx, ty_hbm, tys_hbm,
     out_field, out_k1, out_k2, out_sg,
-    sw, mz, mzs, taps, wide,
+    k1, k2, ty, tys, sw, sg, mz, mzs, taps, wide,
     xe, de, xw, hw, dw, pw, pre, brn, band, cg, zt, sp, dts, dtl,
-    s1, r1, s2, r2, xs, xt, yf, yg, s3, r3, s4, r4, kgf, kgb, r5, s6, r6, s7, r7,
+    s1, r1, s2, r2, xs, xt, dys, yf, yg, s3, r3, s4, r4, kgf, kgb, r5, s6, r6, s7, r7,
     hs, hr, sx, rx, sy, ry, ls,
 ):
-    load_z = pltpu.make_async_copy(mz_hbm, mz, ls.at[0])
-    load_w = pltpu.make_async_copy(sw_hbm, sw, ls.at[1])
-    load_zs = pltpu.make_async_copy(mzs_hbm, mzs, ls.at[2])
-    load_z.start()
-    load_w.start()
-    load_zs.start()
     gx = lax.axis_index("gx")
     gy = lax.axis_index("gy")
+    loads = [
+        pltpu.make_async_copy(k1_hbm, k1, ls.at[0]),
+        pltpu.make_async_copy(k2_hbm, k2, ls.at[1]),
+        pltpu.make_async_copy(ty_hbm.at[gy], ty, ls.at[2]),
+        pltpu.make_async_copy(tys_hbm.at[gy], tys, ls.at[3]),
+        pltpu.make_async_copy(sw_hbm, sw, ls.at[4]),
+    ]
+    for load in loads:
+        load.start()
+
+    zl, px = gx // 4, lax.rem(gx, 4)
+    py, zc = gy // 4, lax.rem(gy, 4)
 
     def around(i, k):
         return lax.rem(i + k + PEERS, PEERS)
@@ -106,6 +114,14 @@
             pl.semaphore_signal(
                 barrier, inc=1, device_id=(around(gx, i), around(gy, j)), device_id_type=MESH
             )
+
+    for i in range(1, 4):
+        for j in range(1, 4):
+            for where in (
+                (zl * 4 + lax.rem(px + i, 4), lax.rem(py + j, 4) * 4 + zc),
+                (lax.rem(zl + i, 4) * 4 + px, py * 4 + lax.rem(zc + j, 4)),
+            ):
+                pl.semaphore_signal(barrier, inc=1, device_id=where, device_id_type=MESH)
 
     sides = [(i, j) for i in (-1, 0, 1) for j in (-1, 0, 1) if (i, j) != (0, 0)]
     x_from = {-1: (2, 2), 0: (2, 4), 1: (4, 2)}
@@ -136,8 +152,17 @@
             rim_copy(ext, which, n, i, j).wait_send()
 
     def exchange(axis, src, dst, which, scatter, n):
-        me = gx if axis == "gx" else gy
-        send, recv = (sx, rx) if axis == "gx" else (sy, ry)
+        me = {"gx": gx, "gy": gy, "xy": px * 4 + py, "z": zl * 4 + zc}[axis]
+        send, recv = (sy, ry) if axis == "gy" else (sx, rx)
+
+        def device(peer):
+            if axis == "gx":
+                return (peer, gy)
+            if axis == "gy":
+                return (gx, peer)
+            if axis == "xy":
+                return (zl * 4 + peer // 4, lax.rem(peer, 4) * 4 + zc)
+            return (peer // 4 * 4 + px, py * 4 + lax.rem(peer, 4))
 
         def copy(k, peer, slot):
             return pltpu.make_async_remote_copy(
@@ -145,7 +170,7 @@
                 dst_ref=dst.at[pl.ds(n * slot, n)],
                 send_sem=send.at[which, k],
                 recv_sem=recv.at[which, k],
-                device_id=(peer, gy) if axis == "gx" else (gx, peer),
+                device_id=device(peer),
                 device_id_type=MESH,
             )
 
@@ -178,6 +203,17 @@
             return acc + dst[pl.ds(n * k, n)].astype(F32)
 
         return lax.fori_loop(0, PEERS, add, jnp.zeros((n,) + dst.shape[1:], F32))
+
+    def spread(table, made, n, width):
+        row = lax.broadcasted_iota(jnp.int32, (C, width), 0)
+        unit = row == lax.rem(lax.broadcasted_iota(jnp.int32, (C, width), 1), C)
+        for part in range(2):
+
+            @pl.loop(0, n)
+            def _(i):
+                wide_row = jnp.broadcast_to(table[part, pl.ds(i, 1), :], (C, width))
+                at = pl.ds(pl.multiple_of(i * C, C), C)
+                made[part, at, :] = jnp.where(unit, wide_row, 0.0).astype(BF16)
 
     def z_modes(rows):
         modes = dot(rows, mz[0]) + dot(rows, mz[1])
@@ -230,7 +266,7 @@
                 straight = jnp.where(lane < 32, re_here, jnp.where(lane < 64, im_after, 0.0))
                 crossed = jnp.where(lane < 32, im_here, jnp.where(lane < 64, -re_after, 0.0))
                 blocks.append(jnp.concatenate([straight, crossed], axis=0))
-        modes = dot(ty[gy], jnp.concatenate(blocks, axis=1), HIGH)
+        modes = dot(ty[...], jnp.concatenate(blocks, axis=1), HIGH)
         for p in range(12):
             at = 128 * p
             rows = modes[0:16, at : at + 128] + pltpu.roll(modes[16:32, at : at + 128], 64, 1)
@@ -256,7 +292,7 @@
                 end = min(9 * d + 9, 12 * p + 12)
                 yg[p, row - 12 * p : end - 12 * p] = r3[which, d, row - 9 * d : end - 9 * d]
                 row = end
-        cells = dot(tys[gy], jnp.concatenate([yg[p] for p in range(12)], axis=1), HIGH)
+        cells = dot(tys[...], jnp.concatenate([yg[p] for p in range(12)], axis=1), HIGH)
         for u in range(3):
             re = jnp.zeros((LY, 128), F32)
             im = jnp.zeros((LY, 128), F32)
@@ -339,7 +375,7 @@
             a, b = a + off, b + off
             rows = src[b % 2, a : a + LX, b // 2 : b // 2 + LY // 2].reshape(256, 256)
             prod = dot(turned, rows)
-            group, place = divmod((q * 9 + ab) * 3, 4)
+            group, place = divmod(ab * 3, 4)
             first_lane = 32 * place
             acc = jnp.zeros((C, 256), F32)
             for zl in range(4):
@@ -347,9 +383,31 @@
                 piece = prod[32 * zl : 32 * zl + 32]
                 acc = acc + (pltpu.roll(piece, shift, 1) if shift else piece)
             acc = jnp.where((lanes >= first_lane) & (lanes < first_lane + 96), acc, 0.0)
-            kgf[32 * group : 32 * group + 32] += acc[:, 0:128]
+            kgf[q, 32 * group : 32 * group + 32] += acc[:, 0:128]
             if first_lane + 96 > 128:
-                kgf[32 * group + 32 : 32 * group + 64] += acc[:, 128:256]
+                kgf[q, 32 * group + 32 : 32 * group + 64] += acc[:, 128:256]
+        for d in range(PEERS):
+            kgb[q, d] = kgf[q, 14 * d : 14 * d + 16].astype(BF16)
+
+    def grad_scatter(q):
+        start, arrived, done = exchange("xy", kgb.at[q], r5.at[q], 4 + q, True, 1)
+        start_all(start)
+        r5[q, px * 4 + py] = kgb[q, px * 4 + py]
+        return arrived, done
+
+    def grad_sum(q):
+        s6[q, 0] = total_of(r5.at[q], 1)[0, 0:14]
+        start, arrived, done = exchange("z", s6.at[q], r6.at[q], 8 + q, False, 1)
+        start_all(start)
+        r6[q, zl * 4 + zc] = s6[q, 0]
+        return arrived, done
+
+    def grad_gather(q):
+        s7[q] = total_of(r6.at[q], 1)
+        start, arrived, done = exchange("xy", s7.at[q], r7.at[q], 6 + q, False, 1)
+        start_all(start)
+        r7[q, px * 4 + py] = s7[q, 0]
+        return arrived, done
 
     def widen(ext, dst):
         @pl.loop(0, 8)
@@ -367,14 +425,15 @@
             sp[8 * x : 8 * x + 8, b, :] = mine[:, 128 * b : 128 * b + 128]
             cg[8 * x : 8 * x + 8, b, :] = g[:, 128 * b : 128 * b + 128]
     xe[2:6, 1:5] = sp[...].reshape(4, 4, 16, 128).astype(BF16)
-    load_z.wait()
+    spread(fz, mz, NZ, 2 * MZ * C)
     z_modes(field[...].reshape(32, 1024))
 
-    pl.semaphore_wait(barrier, 2 * (PEERS - 1) + 4)
+    pl.semaphore_wait(barrier, 2 * (PEERS - 1) + 22)
 
     x_arrived, x_done = x_send(0)
-    rim_send(xe, 0)
-
+
+    for load in loads[:4]:
+        load.wait()
     group = lax.broadcasted_iota(jnp.int32, (C, 128), 1) // C
     for q, kernel in ((0, k1), (1, k2)):
 
@@ -398,28 +457,15 @@
     kgf[...] = jnp.zeros_like(kgf)
     yg[...] = jnp.zeros_like(yg)
 
-    rim_wait(xe, 0)
-    widen(xe, xw)
-    conv(xw, 0, 6, 10, pre)
 
     wait_all(x_arrived)
     y_arrived, y_done = y_send(0)
 
-    @pl.loop(0, 6)
-    def _(i):
-        rows = pl.ds(pl.multiple_of(i * 80, 80), 80)
-        h, slope = gelu_parts(pre[rows])
-        pre[rows] = slope
-        yi = lax.broadcasted_iota(jnp.int32, (10, 8, 128), 0) + (gy * LY - 1)
-        row = gx * LX - 1 + i
-        ok = (row >= 0) & (row < NX) & (yi >= 0) & (yi < NY)
-        h = h.astype(BF16).astype(F32).reshape(10, 8, 128)
-        windows(hw, i, jnp.where(ok, h, 0.0))
-
-    conv(hw, 1, 4, 8, brn)
+    rim_send(xe, 0)
+    spread(fzs, mzs, 2 * MZ, NZ * C)
 
     wait_all(y_arrived)
-    load_w.wait()
+    loads[4].wait()
     first = (gx * PEERS + gy) * 18
 
     def scale_of(m):
@@ -441,9 +487,27 @@
             row.append(jnp.sum(xr * wi + xi * wr, axis=0, keepdims=True) * scale_of(m))
         s3[0, 0, t : t + 1, :] = jnp.concatenate(row, axis=1)
     m_arrived, m_done = modes_send(0)
+
+    rim_wait(xe, 0)
+    widen(xe, xw)
+    conv(xw, 0, 6, 10, pre)
+
     wait_all(m_arrived)
     c_arrived, c_done = columns_send(0)
-    load_zs.wait()
+
+    @pl.loop(0, 6)
+    def _(i):
+        rows = pl.ds(pl.multiple_of(i * 80, 80), 80)
+        h, slope = gelu_parts(pre[rows])
+        pre[rows] = slope
+        yi = lax.broadcasted_iota(jnp.int32, (10, 8, 128), 0) + (gy * LY - 1)
+        row = gx * LX - 1 + i
+        ok = (row >= 0) & (row < NX) & (yi >= 0) & (yi < NY)
+        h = h.astype(BF16).astype(F32).reshape(10, 8, 128)
+        windows(hw, i, jnp.where(ok, h, 0.0))
+
+    conv(hw, 1, 4, 8, brn)
+
     wait_all(c_arrived)
     spectral = cells_of(0)
     for b in range(8):
@@ -459,6 +523,8 @@
     z_modes(dtl[...])
     x_arrived2, x_done2 = x_send(1)
 
+    correlate(hw, 0, dts[...].reshape(256, 128), 1)
+    k_arrived2, k_done2 = grad_scatter(1)
     rim_wait(de, 1)
     widen(de, dw)
     conv(dw, 2, 6, 10, wide)
@@ -472,16 +538,15 @@
         ok = (row >= 0) & (row < NX) & (yi >= 0) & (yi < NY)
         windows(pw, i, jnp.where(ok, dpre, 0.0))
 
+    own = pw[1, 1:5, 0:4, :, 0:128].reshape(256, 128).astype(F32)
+    correlate(xw, 1, own, 0)
+    k_arrived, k_done = grad_scatter(0)
+
     wait_all(x_arrived2)
     y_arrived2, y_done2 = y_send(1)
-
-    correlate(hw, 0, dts[...].reshape(256, 128), 1)
-    correlate(xw, 1, pw[1, 1:5, 0:4, :, 0:128].reshape(256, 128).astype(F32), 0)
-    for d in range(PEERS):
-        kgb[d] = kgf[28 * d : 28 * d + 32].astype(BF16)
-    k_start, k_arrived, k_done = exchange("gx", kgb, r5, 4, True, 1)
-    start_all(k_start)
-    r5[gx] = kgb[gx]
+    wait_all(k_arrived2)
+    l_arrived2, l_done2 = grad_sum(1)
+    conv(pw, 3, 4, 8, brn)
 
     wait_all(y_arrived2)
     xs[0:9] = total_of(r2.at[1], 1)[0]
@@ -489,39 +554,41 @@
     back = jnp.zeros((128, 128), F32)
     for t in range(9):
         column = []
+        dy = xs[t : t + 1, :] * scale_of(2 * t)
+        dys[t : t + 1, :] = dy
         for half in range(2):
             m = 2 * t + half
-            xr = xt[64 * half : 64 * half + 32, t : t + 1]
-            xi = xt[64 * half + 32 : 64 * half + 64, t : t + 1]
             wr = sw[0, m]
             wi = sw[1, m]
-            dy = xs[t : t + 1, :] * scale_of(m)
             dyr = dy[:, 64 * half : 64 * half + 32]
             dyi = dy[:, 64 * half + 32 : 64 * half + 64]
-            out_sg[0, m] = xr * dyr + xi * dyi
-            out_sg[1, m] = xr * dyi - xi * dyr
             column.append(jnp.sum(wr * dyr + wi * dyi, axis=1, keepdims=True))
             column.append(jnp.sum(wr * dyi - wi * dyr, axis=1, keepdims=True))
         back = jnp.where(mode_lane == t, jnp.concatenate(column, axis=0), back)
     xs[...] = back.T
     s3[1, 0] = xs[0:9]
     m_arrived2, m_done2 = modes_send(1)
+    for t in range(9):
+        for half in range(2):
+            m = 2 * t + half
+            xr = xt[64 * half : 64 * half + 32, t : t + 1]
+            xi = xt[64 * half + 32 : 64 * half + 64, t : t + 1]
+            dyr = dys[t : t + 1, 64 * half : 64 * half + 32]
+            dyi = dys[t : t + 1, 64 * half + 32 : 64 * half + 64]
+            sg[0, m] = xr * dyr + xi * dyi
+            sg[1, m] = xr * dyi - xi * dyr
+    save = pltpu.make_async_copy(sg, out_sg, ls.at[5])
+    save.start()
 
     wait_all(k_arrived)
-    s6[0] = total_of(r5, 1)[0, 0:28]
-    l_start, l_arrived, l_done = exchange("gy", s6, r6, 4, False, 1)
-    start_all(l_start)
-    r6[gy] = s6[0]
-    conv(pw, 3, 4, 8, brn)
-
+    l_arrived, l_done = grad_sum(0)
     wait_all(m_arrived2)
     c_arrived2, c_done2 = columns_send(1)
 
+    wait_all(l_arrived2)
+    n_arrived2, n_done2 = grad_gather(1)
     wait_all(l_arrived)
-    s7[...] = total_of(r6, 1)
-    n_start, n_arrived, n_done = exchange("gx", s7, r7, 5, False, 1)
-    start_all(n_start)
-    r7[gx] = s7[0]
+    n_arrived, n_done = grad_gather(0)
 
     wait_all(c_arrived2)
     spectral = cells_of(1)
@@ -529,28 +596,37 @@
     for b in range(8):
         value = spectral[:, 128 * b : 128 * b + 128] + dts[:, b, :]
         out_field[:, :, 128 * b : 128 * b + 128] = value.reshape(LX, LY, 128).astype(BF16)
-    wait_all(n_arrived)
-    for d in range(PEERS):
-        kgf[28 * d : 28 * d + 28] = r7[d]
-    for group in range(14):
-        turned = kgf[32 * group : 32 * group + 32].T
-        for place in range(4):
-            block = 4 * group + place
-            if block < 54:
-                out = out_k1 if block < 27 else out_k2
-                out[block % 27] = turned[32 * place : 32 * place + 32]
-
+    for q, waiting, out in ((1, n_arrived2, out_k2), (0, n_arrived, out_k1)):
+        wait_all(waiting)
+        for d in range(PEERS):
+            kgf[q, 14 * d : 14 * d + 14] = r7[q, d]
+        for group in range(7):
+            turned = kgf[q, 32 * group : 32 * group + 32].T
+            for place in range(min(4, 27 - 4 * group)):
+                out[4 * group + place] = turned[32 * place : 32 * place + 32]
+
+    save.wait()
     rim_done(xe, 0)
     rim_done(de, 1)
     for done in (
-        x_done, y_done, m_done, c_done, x_done2, y_done2, m_done2, c_done2, k_done, l_done, n_done
+        x_done, y_done, m_done, c_done, x_done2, y_done2, m_done2, c_done2, k_done, l_done, n_done,
+        k_done2, l_done2, n_done2,
     ):
         done()
 
 
 def hand_over(*refs):
-    for source, target in zip(refs[:4], refs[4:]):
-        target[...] = source[...]
+    results, outs, kept_here = refs[0:4], refs[4:8], refs[8:12]
+    into, out = refs[12:14]
+    loads = [pltpu.make_async_copy(results[i], kept_here[i], into.at[i]) for i in range(4)]
+    saves = [pltpu.make_async_copy(kept_here[i], outs[i], out.at[i]) for i in range(4)]
+    for load in loads:
+        load.start()
+    for load, save in zip(loads, saves):
+        load.wait()
+        save.start()
+    for save in saves:
+        save.wait()
 
 
 def shards(field, cotangent, kernel_one, kernel_two, spectral_weight):
@@ -570,12 +646,17 @@
             jax.ShapeDtypeStruct((27, C, C), F32),
             jax.ShapeDtypeStruct(spectral_weight.shape, F32),
         ),
-        in_specs=[vmem, vmem, vmem, vmem, hbm, hbm, hbm, smem, vmem, vmem],
-        out_specs=(vmem, vmem, vmem, vmem),
+        in_specs=[vmem, vmem, hbm, hbm, hbm, vmem, vmem, smem, hbm, hbm],
+        out_specs=(vmem, vmem, vmem, hbm),
         scratch_shapes=[
+            buf((27, C, C), BF16),
+            buf((27, C, C), BF16),
+            buf((32, 16)),
+            buf((32, 16)),
             buf(spectral_weight.shape),
-            buf(mz.shape, BF16),
-            buf(mzs.shape, BF16),
+            buf(spectral_weight.shape),
+            buf((2, NZ * C, 2 * MZ * C), BF16),
+            buf((2, 2 * MZ * C, NZ * C), BF16),
             buf((256, 128)),
             buf((480, 128)),
             buf((8, 6, 16, 128), BF16),
@@ -598,26 +679,27 @@
             buf((2, PEERS, 9, 128)),
             buf((128, 128)),
             buf((128, 128)),
+            buf((16, 128)),
             buf((144, 128)),
             buf((12, 16, 128)),
             buf((2, 1, 9, 128)),
             buf((2, PEERS, 9, 128)),
             buf((2, 3, 16, 128), BF16),
             buf((2, 48, 16, 128), BF16),
-            buf((480, 128)),
-            buf((PEERS, 32, 128), BF16),
-            buf((PEERS, 32, 128), BF16),
-            buf((1, 28, 128)),
-            buf((PEERS, 28, 128)),
-            buf((1, 28, 128)),
-            buf((PEERS, 28, 128)),
+            buf((2, 256, 128)),
+            buf((2, PEERS, 16, 128), BF16),
+            buf((2, PEERS, 16, 128), BF16),
+            buf((2, 1, 14, 128)),
+            buf((2, PEERS, 14, 128)),
+            buf((2, 1, 14, 128)),
+            buf((2, PEERS, 14, 128)),
             pltpu.SemaphoreType.DMA((2, 8)),
             pltpu.SemaphoreType.DMA((2, 8)),
-            pltpu.SemaphoreType.DMA((6, PEERS)),
-            pltpu.SemaphoreType.DMA((6, PEERS)),
-            pltpu.SemaphoreType.DMA((5, PEERS)),
-            pltpu.SemaphoreType.DMA((5, PEERS)),
-            pltpu.SemaphoreType.DMA((3,)),
+            pltpu.SemaphoreType.DMA((10, PEERS)),
+            pltpu.SemaphoreType.DMA((10, PEERS)),
+            pltpu.SemaphoreType.DMA((4, PEERS)),
+            pltpu.SemaphoreType.DMA((4, PEERS)),
+            pltpu.SemaphoreType.DMA((6,)),
         ],
         compiler_params=pltpu.CompilerParams(
             collective_id=0, has_side_effects=True, vmem_limit_bytes=56 << 20
@@ -626,8 +708,10 @@
     return pl.pallas_call(
         hand_over,
         out_shape=tuple(jax.ShapeDtypeStruct(r.shape, r.dtype) for r in results),
-        in_specs=[vmem] * 4,
-        out_specs=(vmem,) * 4,
+        in_specs=[hbm] * 4,
+        out_specs=(hbm,) * 4,
+        scratch_shapes=[buf(r.shape, r.dtype) for r in results]
+        + [pltpu.SemaphoreType.DMA((4,)), pltpu.SemaphoreType.DMA((4,))],
     )(*results)
 
 

time: 95.8 us -> 85.1 us (0.89); the launches traced: 94.6 us -> 84.9 us
  Pallas kernels: 93.9 us -> 84.3 us
    pallas_call x1, Pallas kernels: 91.4 us -> 82 us  [shards(): pl.pallas_call(body, out_shape=(jax.ShapeDtypeStruct((LX, LY, NZ * C), BF...]
where the time goes in v3:
time: 85.1 us; the launch traced here: 84.9 us
  Pallas kernels  84.3 us (99%)
    pallas_call x1, Pallas kernels, shards(): pl.pallas_call(body, out_shape=(jax.ShapeDtypeStruct((LX, LY, NZ * C), BF...  82 us
    pallas_call x1, Pallas kernels, shards(): pl.pallas_call(hand_over, out_shape=tuple((jax.ShapeDtypeStruct(r.shape,...  2.25 us

profile of v3, /device:TPU:32, one launch (start us, length us, event | category | flops | bytes accessed | tf_op | source)
XLA Modules:
  0.0 84.9 jit_solution(6890226730520072161)
XLA Ops:
  0.6 82.0 %shard_map.129 = (bf16[4,8,1024]{2,1,0:T(8,128)(2,1)}, f32[27,32,32]{2,1,0:T(8,128)}, f32[27,32,32]{2,1,0:T(8,128)}, f32[2,18,32,32]{3,2,1,0:T(8,128)}) custom-call(bf16[4,8,1024]{2,1,0:T(8,128)(2,1)} %field.1, bf16[4,8,1024]{2,1,0:T(8,128)(2,1)} %cot.1, bf16[27,32,32]{2,1,0:T(8,128)(2,1)} %k1_hbm.1, bf16[27,32,32]{2,1,0:T(8,128)(2,1)} %k2_hbm.1, ...), custom_call_target="tpu_custom_call" | custom-call | tf_op jit(solution)/shard_map/pallas_call | solution.py:641
  82.7 2.3 %shard_map.130 = (bf16[4,8,1024]{2,1,0:T(8,128)(2,1)}, f32[27,32,32]{2,1,0:T(8,128)}, f32[27,32,32]{2,1,0:T(8,128)}, f32[2,18,32,32]{3,2,1,0:T(8,128)}) custom-call(bf16[4,8,1024]{2,1,0:T(8,128)(2,1)} %get-tuple-element.8.refs_0_, f32[27,32,32]{2,1,0:T(8,128)} %get-tuple-element.9.refs_1_, f32[27,32,32]{2,1,0:T(8,128)} %get-tuple-element.10.refs_2_, ...), custom_call_target="tpu_custom_call" | custom-call | tf_op jit(solution)/shard_map/pallas_call | solution.py:708

commit v4 on v3

--- a/solution.py
+++ b/solution.py
@@ -458,11 +458,10 @@
     yg[...] = jnp.zeros_like(yg)
 
 
+    spread(fzs, mzs, 2 * MZ, NZ * C)
     wait_all(x_arrived)
     y_arrived, y_done = y_send(0)
 
-    rim_send(xe, 0)
-    spread(fzs, mzs, 2 * MZ, NZ * C)
 
     wait_all(y_arrived)
     loads[4].wait()
@@ -487,13 +486,14 @@
             row.append(jnp.sum(xr * wi + xi * wr, axis=0, keepdims=True) * scale_of(m))
         s3[0, 0, t : t + 1, :] = jnp.concatenate(row, axis=1)
     m_arrived, m_done = modes_send(0)
-
+    rim_send(xe, 0)
+
+
+    wait_all(m_arrived)
+    c_arrived, c_done = columns_send(0)
     rim_wait(xe, 0)
     widen(xe, xw)
     conv(xw, 0, 6, 10, pre)
-
-    wait_all(m_arrived)
-    c_arrived, c_done = columns_send(0)
 
     @pl.loop(0, 6)
     def _(i):
@@ -547,6 +547,8 @@
     wait_all(k_arrived2)
     l_arrived2, l_done2 = grad_sum(1)
     conv(pw, 3, 4, 8, brn)
+    wait_all(k_arrived)
+    l_arrived, l_done = grad_sum(0)
 
     wait_all(y_arrived2)
     xs[0:9] = total_of(r2.at[1], 1)[0]
@@ -580,8 +582,6 @@
     save = pltpu.make_async_copy(sg, out_sg, ls.at[5])
     save.start()
 
-    wait_all(k_arrived)
-    l_arrived, l_done = grad_sum(0)
     wait_all(m_arrived2)
     c_arrived2, c_done2 = columns_send(1)
 

time: 85.1 us -> 84.4 us (level)
  no operation moved by 1% of the time
where the time goes in v4:
time: 84.4 us; the launch traced here: 84.3 us
  Pallas kernels  83.6 us (99%)
    pallas_call x1, Pallas kernels, shards(): pl.pallas_call(body, out_shape=(jax.ShapeDtypeStruct((LX, LY, NZ * C), BF...  81.4 us
    pallas_call x1, Pallas kernels, shards(): pl.pallas_call(hand_over, out_shape=tuple((jax.ShapeDtypeStruct(r.shape,...  2.25 us

profile of v4, /device:TPU:32, one launch (start us, length us, event | category | flops | bytes accessed | tf_op | source)
XLA Modules:
  0.0 84.3 jit_solution(10046482469539288385)
XLA Ops:
  0.6 81.4 %shard_map.129 = (bf16[4,8,1024]{2,1,0:T(8,128)(2,1)}, f32[27,32,32]{2,1,0:T(8,128)}, f32[27,32,32]{2,1,0:T(8,128)}, f32[2,18,32,32]{3,2,1,0:T(8,128)}) custom-call(bf16[4,8,1024]{2,1,0:T(8,128)(2,1)} %field.1, bf16[4,8,1024]{2,1,0:T(8,128)(2,1)} %cot.1, bf16[27,32,32]{2,1,0:T(8,128)(2,1)} %k1_hbm.1, bf16[27,32,32]{2,1,0:T(8,128)(2,1)} %k2_hbm.1, ...), custom_call_target="tpu_custom_call" | custom-call | tf_op jit(solution)/shard_map/pallas_call | solution.py:641
  82.0 2.3 %shard_map.130 = (bf16[4,8,1024]{2,1,0:T(8,128)(2,1)}, f32[27,32,32]{2,1,0:T(8,128)}, f32[27,32,32]{2,1,0:T(8,128)}, f32[2,18,32,32]{3,2,1,0:T(8,128)}) custom-call(bf16[4,8,1024]{2,1,0:T(8,128)(2,1)} %get-tuple-element.8.refs_0_, f32[27,32,32]{2,1,0:T(8,128)} %get-tuple-element.9.refs_1_, f32[27,32,32]{2,1,0:T(8,128)} %get-tuple-element.10.refs_2_, ...), custom_call_target="tpu_custom_call" | custom-call | tf_op jit(solution)/shard_map/pallas_call | solution.py:708
